TPU v7x, 32 devices: a whole 2x2x4 slice. The times are simulated.
32 devices in a mesh: dom: 16 (over z, y, core), rec: 2 (over x).
Axes of the slice: x: 2, y: 2, z: 4, core: 2. Of those that a mesh axis runs over, the one named last changes fastest.
Arguments:
- features: float32 [16384, 512], P(('dom', 'rec')), may hold values from -6 to 6
- positions: float32 [3, 16384], P(None, ('dom', 'rec')), may hold values from 0 to 2
- value_one: float32 [512, 512], replicated, may hold values from -0.25 to 0.25
- output_one: float32 [512, 512], replicated, may hold values from -0.25 to 0.25
- radial_one: float32 [8, 512], replicated, may hold values from -6 to 6
- value_two: float32 [512, 512], replicated, may hold values from -0.25 to 0.25
- output_two: float32 [512, 512], replicated, may hold values from -0.25 to 0.25
- radial_two: float32 [8, 512], replicated, may hold values from -6 to 6
- charge_weight: float32 [512, 2], replicated, may hold values from -0.25 to 0.25
- return_weight: float32 [2, 512], replicated, may hold values from -4 to 4
- green_kernel: float32 [192, 2, 2, 192, 192], P('rec', None, None, None, 'dom'), may hold values from -24 to 24
- exports: int32 [32, 2, 3], P(('dom', 'rec')), may hold values from 0 to 7, as said below
- export_counts: int32 [32, 2], P(('dom', 'rec')), may hold values from 1 to 3, as said below
- brick_anchor: int32 [3, 256], P(None, ('dom', 'rec')), may hold values from 0 to 188, as said below
Outputs:
- updated: float32 [16384, 512], P(('dom', 'rec'))
Inputs may be any that keep to these rules, and one draw needn't show every extreme that they name: `exports`: each entry names one of the 8 blocks of its own domain, counted from 0; the 3 entries of one domain and side are distinct. `export_counts`: the live entries of a list are its first ones. `brick_anchor`: A block's brick of 4 x 8 x 8 cells lies inside the grid, and its first coordinates lie within the planes of the grid's first dimension that the dom index holding the block holds.
All inputs are finite; a program needn't handle non-finite values.
Results may differ from a plain program's by a relative error of at most 0.0003.
Values sent between devices are 32-bit elements; how exact they have to be, the bound alone decides.
No kernel may reach another device: no remote copies, remote signals or barrier semaphores. Data moves between devices by JAX's collectives and lax.ppermute only.
A program may use at most 128 MiB of HBM per device.

v0:
```python
import math

import jax
import jax.numpy as jnp
from jax import lax
from jax.sharding import PartitionSpec as P

BA = 64
BX = 4
BY = 8
BZ = 8


exact_mode = lax.Precision.HIGHEST
sharp_factor = 2.0
radial_reach = 3.0
soften = 0.01
norm_epsilon = 1e-05


def passed_along(shard, axis, by):
    length = lax.axis_size(axis)
    return lax.ppermute(shard, axis, [(i, (i + by) % length) for i in range(length)])


def radial_basis(squared, levels):
    centers = jnp.arange(levels, dtype=jnp.float32) * (radial_reach / (levels - 1))
    distance = jnp.sqrt(squared + soften)
    shaped = centers.reshape((levels,) + (1,) * squared.ndim)
    return jnp.exp(-sharp_factor * (distance[None] - shaped) ** 2)


def block_messages(own_values, own_places, ghost_values, ghost_places, live_atoms, radial_weight):
    blocks = own_values.shape[0]
    members = own_values.shape[1]
    partner_values = jnp.concatenate(
        [own_values, jnp.broadcast_to(ghost_values[None], (blocks,) + ghost_values.shape)], axis=1
    )
    partner_places = jnp.concatenate(
        [own_places, jnp.broadcast_to(ghost_places[:, None], (3, blocks, ghost_places.shape[1]))],
        axis=2,
    )
    squared = jnp.sum((own_places[:, :, :, None] - partner_places[:, :, None, :]) ** 2, axis=0)
    kept_pairs = jnp.concatenate(
        [
            1.0 - jnp.eye(members, dtype=jnp.float32),
            jnp.broadcast_to(live_atoms[None], (members, live_atoms.shape[0])),
        ],
        axis=1,
    )
    radial_terms = radial_basis(squared, radial_weight.shape[0]) * kept_pairs
    gathered = jnp.einsum("kbip,bpf->kbif", radial_terms, partner_values, precision=exact_mode)
    return jnp.einsum("kbif,kf->bif", gathered, radial_weight, precision=exact_mode)


def ghost_blocks(values, places, exports, export_counts):
    blocks = values.shape[0] // BA
    features_count = values.shape[1]
    slot_count = exports.shape[2]
    value_blocks = values.reshape(blocks, BA, features_count)
    place_blocks = places.reshape(3, blocks, BA)
    slot_index = jnp.arange(slot_count, dtype=jnp.int32)
    got_values, got_places, got_live = ([], [], [])
    for shift_by, side_index in ((1, 0), (-1, 1)):
        chosen = exports[0, side_index]
        count_here = export_counts[0, side_index]
        packed = (
            value_blocks[chosen].reshape(slot_count * BA, features_count),
            place_blocks[:, chosen].reshape(3, slot_count * BA),
            (slot_index < count_here).astype(jnp.float32),
        )
        far_values, far_places, far_live = passed_along(
            (packed[0], packed[1], packed[2]), ("dom", "rec"), shift_by
        )
        got_values.append(far_values)
        got_places.append(far_places)
        got_live.append(far_live)
    return (
        jnp.concatenate(got_values, axis=0),
        jnp.concatenate(got_places, axis=1),
        jnp.repeat(jnp.concatenate(got_live), BA),
    )


def interaction(hidden, places, value_weight, output_weight, radial_weight, exports, export_counts):
    values = jnp.dot(hidden, value_weight, precision=exact_mode, preferred_element_type=jnp.float32)
    ghost_values, ghost_places, live_atoms = ghost_blocks(values, places, exports, export_counts)
    blocks = values.shape[0] // BA
    messages = block_messages(
        values.reshape(blocks, BA, values.shape[1]),
        places.reshape(3, blocks, BA),
        ghost_values,
        ghost_places,
        live_atoms,
        radial_weight,
    ).reshape(values.shape)
    scaled = messages * lax.rsqrt(
        jnp.mean(messages * messages, axis=-1, keepdims=True) + norm_epsilon
    )
    return hidden + jnp.dot(
        jax.nn.silu(scaled), output_weight, precision=exact_mode, preferred_element_type=jnp.float32
    )


def spline_window(coordinate, extent):
    cells = jnp.arange(extent, dtype=jnp.float32)[:, None]
    return jnp.exp(-((cells - coordinate[None] * ((extent - 1) / 2.0)) ** 2))


def dft_tables(count, length):
    row_index = jnp.arange(count, dtype=jnp.int32)
    column_index = jnp.arange(length, dtype=jnp.int32)
    phase = (row_index[:, None] * column_index[None, :] % length).astype(jnp.float32) * (
        2.0 * math.pi / length
    )
    return (jnp.cos(phase), jnp.sin(phase))


def reciprocal(features, places, charge_weight, green_kernel, brick_anchor):
    grid_size = green_kernel.shape[3]
    depth_rows = green_kernel.shape[0]
    slab_depth = grid_size // lax.axis_size("dom")
    blocks = features.shape[0] // BA
    charges = jnp.einsum("af,fc->ca", features, charge_weight, precision=exact_mode)
    along_x = spline_window(places[0], BX)
    along_y = spline_window(places[1], BY)
    along_z = spline_window(places[2], BZ)
    left_side = (charges[:, None] * along_x[None]).reshape(2 * BX, blocks, BA)
    right_side = (along_y[:, None] * along_z[None]).reshape(BY * BZ, blocks, BA)
    bricks = jnp.einsum("pba,qba->bpq", left_side, right_side, precision=exact_mode).reshape(
        blocks, 2, BX, BY, BZ
    )
    anchor_zero = jnp.zeros((), jnp.int32)

    def corner_of(index):
        return (
            anchor_zero,
            brick_anchor[0, index] % slab_depth,
            brick_anchor[1, index],
            brick_anchor[2, index],
        )

    def deposit(index, slab):
        corner = corner_of(index)
        return lax.dynamic_update_slice(
            slab, lax.dynamic_slice(slab, corner, (2, BX, BY, BZ)) + bricks[index], corner
        )

    charge_slab = lax.fori_loop(
        0, blocks, deposit, jnp.zeros((2, slab_depth, grid_size, grid_size), jnp.float32)
    )
    cos_full, sin_full = dft_tables(grid_size, grid_size)
    cosines, sines = dft_tables(depth_rows * lax.axis_size("rec"), grid_size)
    real_part = jnp.einsum("cxyz,kz->kcxy", charge_slab, cosines, precision=exact_mode)
    imag_part = -jnp.einsum("cxyz,kz->kcxy", charge_slab, sines, precision=exact_mode)
    spectrum = lax.psum_scatter(
        jnp.stack([real_part, imag_part], axis=1), "rec", scatter_dimension=0, tiled=True
    )
    real_part, imag_part = (spectrum[:, 0], spectrum[:, 1])
    second_real = jnp.einsum(
        "zcxy,yk->zcxk", real_part, cos_full, precision=exact_mode
    ) + jnp.einsum("zcxy,yk->zcxk", imag_part, sin_full, precision=exact_mode)
    second_imag = jnp.einsum(
        "zcxy,yk->zcxk", imag_part, cos_full, precision=exact_mode
    ) - jnp.einsum("zcxy,yk->zcxk", real_part, sin_full, precision=exact_mode)
    columns = lax.all_to_all(
        jnp.stack([second_real, second_imag], axis=1),
        "dom",
        split_axis=4,
        concat_axis=3,
        tiled=True,
    )
    real_part, imag_part = (columns[:, 0], columns[:, 1])
    first_real = jnp.einsum(
        "zcxk,xm->zcmk", real_part, cos_full, precision=exact_mode
    ) + jnp.einsum("zcxk,xm->zcmk", imag_part, sin_full, precision=exact_mode)
    first_imag = jnp.einsum(
        "zcxk,xm->zcmk", imag_part, cos_full, precision=exact_mode
    ) - jnp.einsum("zcxk,xm->zcmk", real_part, sin_full, precision=exact_mode)
    mixed_real = jnp.einsum("zcdmk,zdmk->zcmk", green_kernel, first_real, precision=exact_mode)
    mixed_imag = jnp.einsum("zcdmk,zdmk->zcmk", green_kernel, first_imag, precision=exact_mode)
    back_real = jnp.einsum(
        "zcmk,mx->zcxk", mixed_real, cos_full, precision=exact_mode
    ) - jnp.einsum("zcmk,mx->zcxk", mixed_imag, sin_full, precision=exact_mode)
    back_imag = jnp.einsum(
        "zcmk,mx->zcxk", mixed_real, sin_full, precision=exact_mode
    ) + jnp.einsum("zcmk,mx->zcxk", mixed_imag, cos_full, precision=exact_mode)
    slabs = lax.all_to_all(
        jnp.stack([back_real, back_imag], axis=1), "dom", split_axis=3, concat_axis=4, tiled=True
    )
    real_part, imag_part = (slabs[:, 0], slabs[:, 1])
    plane_real = jnp.einsum(
        "zcxk,ky->zcxy", real_part, cos_full, precision=exact_mode
    ) - jnp.einsum("zcxk,ky->zcxy", imag_part, sin_full, precision=exact_mode)
    plane_imag = jnp.einsum(
        "zcxk,ky->zcxy", real_part, sin_full, precision=exact_mode
    ) + jnp.einsum("zcxk,ky->zcxy", imag_part, cos_full, precision=exact_mode)
    planes = jnp.stack([plane_real, plane_imag], axis=1)
    piece = lax.all_gather(planes, "rec", axis=0, tiled=True)
    cosines, sines = dft_tables(piece.shape[0], grid_size)
    summed = jnp.einsum("kcxy,kz->cxyz", piece[:, 0], cosines, precision=exact_mode) - jnp.einsum(
        "kcxy,kz->cxyz", piece[:, 1], sines, precision=exact_mode
    )
    potential_slab = summed * (1.0 / float(grid_size) ** 3)

    def brick_at(index):
        return lax.dynamic_slice(potential_slab, corner_of(index), (2, BX, BY, BZ))

    picked = jax.vmap(brick_at)(jnp.arange(blocks, dtype=jnp.int32)).reshape(blocks, 2, BX, BY * BZ)
    partial_sums = jnp.einsum("bcxq,qba->bcxa", picked, right_side, precision=exact_mode)
    return jnp.einsum(
        "bcxa,xba->cba", partial_sums, along_x.reshape(BX, blocks, BA), precision=exact_mode
    ).reshape(2, features.shape[0])


def per_device(
    features,
    positions,
    value_one,
    output_one,
    radial_one,
    value_two,
    output_two,
    radial_two,
    charge_weight,
    return_weight,
    green_kernel,
    exports,
    export_counts,
    brick_anchor,
):
    hidden_one = interaction(
        features, positions, value_one, output_one, radial_one, exports, export_counts
    )
    atom_potential = reciprocal(features, positions, charge_weight, green_kernel, brick_anchor)
    layer_input = hidden_one + jnp.einsum(
        "ca,cf->af", atom_potential, return_weight, precision=exact_mode
    )
    return interaction(
        layer_input, positions, value_two, output_two, radial_two, exports, export_counts
    )


def solution(mesh):
    placed = (
        P(("dom", "rec"), None),
        P(None, ("dom", "rec")),
        P(),
        P(),
        P(),
        P(),
        P(),
        P(),
        P(),
        P(),
        P("rec", None, None, None, "dom"),
        P(("dom", "rec"), None, None),
        P(("dom", "rec"), None),
        P(None, ("dom", "rec")),
    )
    return jax.shard_map(
        per_device, mesh=mesh, in_specs=placed, out_specs=P(("dom", "rec"), None), check_vma=False
    )
```

profile of v0, /device:TPU:0, one launch (start us, length us, event | category | flops | bytes accessed | tf_op | source)
XLA Modules:
  0.0 836.0 jit_solution(5588514848107843732)
XLA Ops:
  13.9 80.4 %while.16 = (s32[]{:T(128)}, f32[2,12,192,192]{3,2,1,0:T(8,128)}, s32[3,8]{1,0:T(4,128)S(1)}, f32[8,2,4,8,8]{4,3,2,1,0:T(8,128)S(1)}, s32[]{:T(128)}, /*index=5*/s32[1,1]{1,0:T(1,128)}, s32[]{:T(128)}, s32[]{:T(128)}, s32[]{:T(128)}) while((s32[]{:T(128)}, f32[2,12,192,192]{3,2,1,0:T(8,128)}, s32[3,8]{1,0:T(4,128)S(1)}, ...), condition=%wide.region_3.4_spmd, body=%wide.region_2.3_spmd.sunk | while | flops 529 | bytes 10541 | solution.py:149
  20.1 3.3 dynamic_update_slice.11
  29.7 4.0 dynamic_update_slice.11
  39.9 4.0 dynamic_update_slice.11
  50.1 4.0 dynamic_update_slice.11
  60.3 4.0 dynamic_update_slice.11
  70.6 4.0 dynamic_update_slice.11
  80.7 3.3 dynamic_update_slice.11
  90.3 4.0 dynamic_update_slice.11
  94.3 7.9 convolution_bitcast_fusion
  102.2 5.4 negate_bitcast_fusion
  107.6 4.7 pad_maximum_fusion
  112.6 113.6 %reduce-scatter.2.cloned.1.call-done = f32[96,2,2,12,192]{4,0,3,2,1:T(8,128)} async-done(((f32[192,2,2,12,192]{4,0,3,2,1:T(8,128)}), f32[96,2,2,12,192]{4,0,3,2,1:T(8,128)}) %reduce-scatter.2.cloned.1.call-update) | async-done | bytes 3538960 | tf_op jit(solution)/shard_map/reduce_scatter | solution.py:156
  226.2 4.6 fusion.43
  242.2 8.2 copy.123
  250.4 109.1 %all_to_all.36 = f32[96,2,2,12,192]{0,2,3,1,4:T(2,128)S(1)} all-to-all(f32[96,2,2,12,192]{0,2,3,1,4:T(2,128)} %copy.123), channel_id=1, replica_groups=mesh['dom'=16,'rec'=2] {'dom'}, dimensions={4} | all-to-all | bytes 7077888 | tf_op jit(solution)/shard_map/all_to_all | solution.py:166
  362.1 3.8 fusion.260
  368.9 6.8 fusion.34
  375.7 6.8 fusion.36
  385.5 8.8 %subtract_bitcast_fusion.2 = f32[96,192,12,2]{0,1,2,3:T(8,128)} fusion(f32[192,96,2,12]{1,0,3,2:T(8,128)} %fusion.34, f32[96,1,2,192,12]{3,0,4,2,1:T(8,128)S(1)} %copy.205), kind=kOutput, calls=%fused_computation.79 | convolution fusion | flops 1019990016 | bytes 5308416 | tf_op jit(solution)/shard_map/zcxk,xm->zcmk/dot_general | solution.py:179
  394.3 4.4 copy.212
  398.7 8.6 %add_bitcast_fusion.2 = f32[96,192,12,2]{0,1,2,3:T(8,128)} fusion(f32[192,96,2,12]{1,0,3,2:T(8,128)} %fusion.36, f32[96,1,2,192,12]{3,0,4,2,1:T(8,128)S(1)} %copy.205), kind=kOutput, calls=%fused_computation.80 | convolution fusion | flops 1019990016 | bytes 5308416 | tf_op jit(solution)/shard_map/zcxk,xm->zcmk/dot_general | solution.py:174
  407.3 4.6 copy.211
  411.9 15.9 %multiply_reduce_fusion.1 = (f32[96,192,12,2]{1,2,3,0:T(8,128)S(1)}, f32[96,192,12,2]{1,2,3,0:T(8,128)S(1)}) fusion(f32[96,2,2,192,12]{3,2,4,1,0:T(2,128)} %param.26, f32[96,192,12,2]{1,3,2,0:T(2,128)} %copy.211, f32[96,192,12,2]{1,3,2,0:T(2,128)S(1)} %copy-done.5), kind=kLoop, calls=%fused_computation.37 | loop fusion | flops 2654208 | bytes 10616832
  427.8 6.3 fusion.28
  434.1 6.7 fusion.26
  440.8 6.3 subtract_bitcast_fusion.1
  447.2 6.5 add_bitcast_fusion.1
  454.0 3.6 copy.136
  457.7 108.6 %all_to_all.37 = f32[96,2,2,192,12]{0,2,4,1,3:T(2,128)S(1)} all-to-all(f32[96,2,2,192,12]{0,2,4,1,3:T(2,128)S(1)} %copy.136), channel_id=1, replica_groups=mesh['dom'=16,'rec'=2] {'dom'}, dimensions={3} | all-to-all | bytes 7077888 | tf_op jit(solution)/shard_map/all_to_all | solution.py:188
  574.4 4.2 fusion.20
  578.6 4.2 fusion.18
  582.8 3.2 copy.207
  586.0 4.7 subtract_bitcast_fusion
  600.4 4.8 collective-permute-start.3
  609.8 5.3 collective-permute-start.1
  629.8 7.0 collective-permute-start.5
  645.6 15.7 %fusion.1 = f32[512,8,64]{0,2,1:T(8,128)S(1)} fusion(f32[512,8]{0,1:T(8,128)S(1)} %bitcast.301, f32[64,448]{1,0:T(8,128)S(1)} %pad_maximum_fusion.6, f32[8]{0:T(128)S(1)} %copy-done.26, f32[8,64,448]{2,1,0:T(8,128)S(1)} %add_sqrt_fusion, f32[8,384,512]{2,1,0:T(8,128)S(1)} %broadcast_in_dim.14, f32[8,64,512]{2,1,0:T(8,128)S(1)} %bitcast.286), kind=kOutput, calls=%fused_computation.19 | convolution fusion | flops 11287396352 | bytes 9437216 | tf_op jit(solution)/shard_map/kbip,bpf->kbif/dot_general | solution.py:52
  661.7 3.2 convolution_add_fusion.2
  665.0 62.2 %all-gather.2.cloned.1.call-done = f32[192,2,2,12,192]{4,0,3,2,1:T(8,128)} async-done(((f32[96,2,2,12,192]{4,0,3,2,1:T(8,128)}), f32[192,2,2,12,192]{4,0,3,2,1:T(8,128)}) %all-gather.2.cloned.1.call-update) | async-done | bytes 7077904 | tf_op jit(solution)/shard_map/all_gather | solution.py:199
  727.2 12.2 %fusion.8 = f32[2,12,192,192]{3,2,1,0:T(8,128)S(1)} fusion(f32[192,2,2,12,192]{4,0,3,2,1:T(8,128)} %all-gather.2.cloned.1.call-done), kind=kOutput, calls=%fused_computation.30 | convolution fusion | flops 2038763520 | bytes 8257536 | tf_op jit(solution)/shard_map/kcxy,kz->cxyz/dot_general | solution.py:201
  739.5 11.7 %subtract_multiply_fusion = f32[2,12,192,192]{3,2,1,0:T(8,128)} fusion(f32[2,12,192,192]{3,2,1,0:T(8,128)S(1)} %fusion.8, f32[192,2,2,12,192]{4,0,3,2,1:T(8,128)S(1)} %copy-done.3), kind=kOutput, calls=%fused_computation.38 | convolution fusion | flops 2040532992 | bytes 12976128 | tf_op jit(solution)/shard_map/kcxy,kz->cxyz/dot_general | solution.py:201
  751.2 28.5 %while.17 = (s32[]{:T(128)}, f32[2,12,192,192]{3,2,1,0:T(8,128)}, s32[8,4]{0,1:T(4,128)S(1)}, f32[8,2,4,8,8]{4,3,2,1,0:T(8,128)S(1)}, s32[]{:T(128)}) while((s32[]{:T(128)}, f32[2,12,192,192]{3,2,1,0:T(8,128)}, s32[8,4]{0,1:T(4,128)S(1)}, f32[8,2,4,8,8]{4,3,2,1,0:T(8,128)S(1)}, s32[]{:T(128)}) %tuple.78), condition=%wide.while_cond, body=%wide.while_body.sunk | while | flops 2 | bytes 34953 | solution.py:207
  786.7 5.3 collective-permute-start.7
  792.0 8.6 %collective-permute-done.6 = f32[192,512]{1,0:T(8,128)S(1)} collective-permute-done((f32[192,512]{1,0:T(8,128)}, f32[192,512]{1,0:T(8,128)S(1)}, u32[]{:S(2)}, u32[]{:S(2)}) %collective-permute-start.6) | collective-permute-done | bytes 393248 | tf_op jit(solution)/shard_map/ppermute | solution.py:23
  800.7 6.0 collective-permute-done.7
  807.9 16.4 %fusion = f32[512,8,64]{0,2,1:T(8,128)S(1)} fusion(f32[512,8]{0,1:T(8,128)S(1)} %bitcast.302, f32[64,448]{1,0:T(8,128)S(1)} %copy-done.16, f32[8]{0:T(128)S(1)} %copy-done.26, f32[8,64,448]{2,1,0:T(8,128)S(1)} %copy-done.13, f32[8,384,512]{2,1,0:T(8,128)S(1)} %broadcast_in_dim.20, f32[8,64,512]{2,1,0:T(8,128)} %bitcast.289), kind=kOutput, calls=%fused_computation.17 | convolution fusion | flops 11287396352 | bytes 9437216 | tf_op jit(solution)/shard_map/kbip,bpf->kbif/dot_general | solution.py:52
  824.7 4.2 convolution_add_fusion
  (196 shorter events, 124.1 us)
Async XLA Ops:
  6.5 598.6 %copy-start = (f32[512,512]{1,0:T(8,128)S(1)}, f32[512,512]{1,0:T(8,128)}, u32[]{:S(2)}) copy-start(f32[512,512]{1,0:T(8,128)} %param.18) | copy-start | bytes 3145732
  6.5 219.6 %reduce-scatter.2.cloned.1.call-start = ((), (), s32[]{:S(2)}) async-start(), calls=%async_computation.3 | async-start | bytes 14155776 | tf_op jit(solution)/shard_map/reduce_scatter | solution.py:156
  8.1 5.8 copy-start.10
  8.1 5.8 copy-start.1
  94.3 7.9 slice-start
  94.3 7.9 slice-start.1
  112.3 614.8 %all-gather.2.cloned.1.call-start = ((), (), s32[]{:S(2)}) async-start(), calls=%async_computation.4 | async-start | bytes 14155776 | tf_op jit(solution)/shard_map/all_gather | solution.py:199
  226.2 4.7 copy-start.2
  407.3 4.6 copy-start.5
  586.0 4.7 copy-start.4
  596.4 0.7 copy-start.19
  596.4 0.8 copy-start.23
  596.4 8.7 %copy-start.6 = (f32[512,512]{1,0:T(8,128)S(1)}, f32[512,512]{1,0:T(8,128)}, u32[]{:S(2)}) copy-start(f32[512,512]{1,0:T(8,128)} %param.16) | copy-start | bytes 3145732
  597.3 3.1 copy-start.20
  597.3 11.1 %copy-start.21 = (s32[1024]{0:T(1024)}, s32[1024]{0:T(1024)S(1)}, u32[]{:S(2)}) copy-start(s32[1024]{0:T(1024)S(1)} %get-tuple-element.164) | copy-start | bytes 12292
  598.5 42.9 %collective-permute-start.2 = (f32[3,192]{1,0:T(4,128)}, f32[3,192]{1,0:T(4,128)}, u32[]{:S(2)}, u32[]{:S(2)}) collective-permute-start(f32[3,192]{1,0:T(4,128)} %reshape.340), channel_id=1, source_target_pairs={{0,1},{1,2},{2,3},{3,4},{4,5},{5,6},{6,7},{7,8},{8,9},{9,10},{10,1... | collective-permute-start | bytes 6920 | tf_op jit(solution)/shard_map/ppermute | solution.py:23
  600.4 41.0 %collective-permute-start.3 = (f32[3,192]{1,0:T(4,128)}, f32[3,192]{1,0:T(4,128)}, u32[]{:S(2)}, u32[]{:S(2)}) collective-permute-start(f32[3,192]{1,0:T(4,128)} %reshape.341), channel_id=1, source_target_pairs={{0,31},{1,0},{2,1},{3,2},{4,3},{5,4},{6,5},{7,6},{8,7},{9,8},{10,9... | collective-permute-start | bytes 6920 | tf_op jit(solution)/shard_map/ppermute | solution.py:23
  607.0 36.0 %copy-start.7 = (f32[512,512]{1,0:T(8,128)}, f32[512,512]{1,0:T(8,128)S(1)}, u32[]{:S(2)}) copy-start(f32[512,512]{1,0:T(8,128)S(1)} %fusion.262) | copy-start | bytes 3145732
  608.4 34.6 %collective-permute-start = (f32[192,512]{1,0:T(8,128)}, f32[192,512]{1,0:T(8,128)S(1)}, u32[]{:S(2)}, u32[]{:S(2)}) collective-permute-start(f32[192,512]{1,0:T(8,128)} %bitcast.292), channel_id=1, source_target_pairs={{0,1},{1,2},{2,3},{3,4},{4,5},{5,6},{6,7},{7,8},{8,9},{9,10},{10,1... | collective-permute-start | bytes 1179656 | tf_op jit(solution)/shard_map/ppermute | solution.py:23
  609.8 33.2 %collective-permute-start.1 = (f32[192,512]{1,0:T(8,128)}, f32[192,512]{1,0:T(8,128)}, u32[]{:S(2)}, u32[]{:S(2)}) collective-permute-start(f32[192,512]{1,0:T(8,128)} %bitcast.293), channel_id=1, source_target_pairs={{0,31},{1,0},{2,1},{3,2},{4,3},{5,4},{6,5},{7,6},{8,7},{9,8},{10,9... | collective-permute-start | bytes 1179656 | tf_op jit(solution)/shard_map/ppermute | solution.py:23
  617.5 12.3 %collective-permute-start.4 = (f32[3]{0:T(128)}, f32[3]{0:T(128)}, u32[]{:S(2)}, u32[]{:S(2)}) collective-permute-start(f32[3]{0:T(128)} %compare_convert_fusion.1), channel_id=1, source_target_pairs={{0,1},{1,2},{2,3},{3,4},{4,5},{5,6},{6,7},{7,8},{8,9},{9,10},{10,1... | collective-permute-start | bytes 44 | tf_op jit(solution)/shard_map/ppermute | solution.py:23
  629.8 8.6 %collective-permute-start.5 = (f32[3]{0:T(128)S(1)}, f32[3]{0:T(128)S(1)}, u32[]{:S(2)}, u32[]{:S(2)}) collective-permute-start(f32[3]{0:T(128)S(1)} %compare_convert_fusion), channel_id=1, source_target_pairs={{0,31},{1,0},{2,1},{3,2},{4,3},{5,4},{6,5},{7,6},{8,7},{9,8},{10,9... | collective-permute-start | bytes 44 | tf_op jit(solution)/shard_map/ppermute | solution.py:23
  641.4 3.9 copy-start.15
  643.0 2.3 copy-start.12
  644.4 1.2 copy-start.8
  644.4 1.2 copy-start.24
  644.4 1.2 copy-start.26
  727.2 12.2 %copy-start.3 = (f32[192,2,2,12,192]{4,0,3,2,1:T(8,128)S(1)}, f32[192,2,2,12,192]{4,0,3,2,1:T(8,128)}, u32[]{:S(2)}) copy-start(f32[192,2,2,12,192]{4,0,3,2,1:T(8,128)} %all-gather.2.cloned.1.call-done) | copy-start | bytes 21233668
  739.4 11.8 %copy-start.14 = (f32[8,2,4,8,8]{4,3,2,1,0:T(8,128)S(1)}, f32[8,2,4,8,8]{4,3,2,1,0:T(8,128)}, u32[]{:S(2)}) copy-start(f32[8,2,4,8,8]{4,3,2,1,0:T(8,128)} %custom-call.18) | copy-start | bytes 49156
  739.4 11.8 %copy-start.17 = (s32[8,4]{0,1:T(4,128)S(1)}, s32[8,4]{0,1:T(4,128)}, u32[]{:S(2)}) copy-start(s32[8,4]{0,1:T(4,128)} %pad_add_fusion) | copy-start | bytes 388
  739.4 40.4 %copy-start.11 = (f32[64,8,64]{2,1,0:T(8,128)S(1)}, f32[64,8,64]{2,1,0:T(8,128)}, u32[]{:S(2)}) copy-start(f32[64,8,64]{2,1,0:T(8,128)} %copy-done.10) | copy-start | bytes 393220
  739.4 40.4 %copy-start.18 = (f32[8,64,4]{1,2,0:T(4,128)S(1)}, f32[8,64,4]{1,2,0:T(4,128)}, u32[]{:S(2)}) copy-start(f32[8,64,4]{1,2,0:T(4,128)} %copy.210) | copy-start | bytes 24580
  739.4 40.9 %copy-start.22 = (f32[2,512]{1,0:T(2,128)S(1)}, f32[2,512]{1,0:T(2,128)}, u32[]{:S(2)}) copy-start(f32[2,512]{1,0:T(2,128)} %param.25) | copy-start | bytes 12292
  784.4 23.1 %copy-start.9 = (f32[512,512]{1,0:T(8,128)}, f32[512,512]{1,0:T(8,128)S(1)}, u32[]{:S(2)}) copy-start(f32[512,512]{1,0:T(8,128)S(1)} %fusion.264) | copy-start | bytes 3145732
  786.6 14.0 %collective-permute-start.6 = (f32[192,512]{1,0:T(8,128)}, f32[192,512]{1,0:T(8,128)S(1)}, u32[]{:S(2)}, u32[]{:S(2)}) collective-permute-start(f32[192,512]{1,0:T(8,128)} %bitcast.295), channel_id=1, source_target_pairs={{0,1},{1,2},{2,3},{3,4},{4,5},{5,6},{6,7},{7,8},{8,9},{9,10},{10,1... | collective-permute-start | bytes 1179656 | tf_op jit(solution)/shard_map/ppermute | solution.py:23
  786.7 20.0 %collective-permute-start.7 = (f32[192,512]{1,0:T(8,128)S(1)}, f32[192,512]{1,0:T(8,128)S(1)}, u32[]{:S(2)}, u32[]{:S(2)}) collective-permute-start(f32[192,512]{1,0:T(8,128)S(1)} %bitcast.294), channel_id=1, source_target_pairs={{0,31},{1,0},{2,1},{3,2},{4,3},{5,4},{6,5},{7,6},{8,7},{9,8},{10,9... | collective-permute-start | bytes 1179656 | tf_op jit(solution)/shard_map/ppermute | solution.py:23
  806.7 1.2 copy-start.13
  806.7 1.2 copy-start.16
  806.7 1.2 copy-start.25
Sparse Core Ops, SparseCore 0:
  112.5 113.6 reduce-scatter.1
  596.6 130.5 all-gather.1
where the time goes:
time: 847 us; the launch traced here: 836 us
  blocking collectives  218 us (26%)
  waiting for transfers between devices  195 us (23%)
  matrix products  172 us (20%)
  local copies, waits for them, and re-layouts  131 us (15%)
  other arithmetic  46.1 us (5%)
  loops' own time  36.8 us (4%)
  starting transfers between devices  23.3 us (3%)
  between operations  14.3 us (2%)
    reduce_scatter x1, waiting for transfers between devices, reciprocal(): lax.psum_scatter(jnp.stack([real_part, imag_part], axis=1), 'rec', scatte...  114 us
    all_to_all x1, blocking collectives, reciprocal(): lax.all_to_all(jnp.stack([second_real, second_imag], axis=1), 'dom', spli...  109 us
    all_to_all x1, blocking collectives, reciprocal(): lax.all_to_all(jnp.stack([back_real, back_imag], axis=1), 'dom', split_ax...  109 us
    all_gather x1, waiting for transfers between devices, reciprocal(): piece = lax.all_gather(planes, 'rec', axis=0, tiled=True)  62.2 us
    another operation x1, loops' own time, reciprocal(): lax.fori_loop(0, blocks, deposit, jnp.zeros((2, slab_depth, grid_size, gr...  36.6 us
    dot_general x2, matrix products, block_messages(): jnp.einsum('kbip,bpf->kbif', radial_terms, partner_values, precision=exac...  32 us
    dynamic_update_slice x8, local copies, waits for them, and re-layouts, deposit(): lax.dynamic_update_slice(slab, lax.dynamic_slice(slab, corner, (2, BX, BY...  30.5 us
    gather x24, local copies, waits for them, and re-layouts  28.3 us
  transfers between devices with their start and end apart: 10, of which 6 were waited for; matrix products, arithmetic and copies ran while one was open for 5% of the time, Pallas kernels for 0%

commit v1 on v0

v1 whole, which is shorter than its diff:
```python
import functools
import math

import jax
import jax.numpy as jnp
import numpy as np
from jax import lax
from jax.experimental import pallas as pl
from jax.experimental.pallas import tpu as pltpu
from jax.sharding import PartitionSpec as P

BA = 64
BX = 4
BY = 8
BZ = 8
NB = 8
NH = 3
NR = 8
LANES = 128

soften = 0.01
norm_epsilon = 1e-05
f32 = jnp.float32
bf16 = jnp.bfloat16
NN = (((1,), (0,)), ((), ()))
NT = (((1,), (1,)), ((), ()))
STEP = 12.0 / 7.0
FACTORS = np.exp(-18.0 * np.arange(NR) ** 2 / 49.0).astype(np.float32)


def params(mib=60):
    return pltpu.CompilerParams(vmem_limit_bytes=mib * 1024 * 1024)


def split(value):
    high = value.astype(bf16)
    return high, (value - high.astype(f32)).astype(bf16)


def product(left, right, dims=NN):
    def one(a, b):
        return lax.dot_general(a, b, dims, preferred_element_type=f32)

    return one(left[0], right[0]) + (one(left[0], right[1]) + one(left[1], right[0]))


def wave(phase, period):
    rest = phase - period * jnp.floor(phase * (1.0 / period) + 0.5)
    turn = rest * (1.0 / period)
    square = turn * turn
    cosine = jnp.full_like(turn, (-1) ** 9 * (2 * math.pi) ** 18 / math.factorial(18))
    sine = jnp.full_like(turn, (-1) ** 9 * (2 * math.pi) ** 19 / math.factorial(19))
    for n in range(8, -1, -1):
        cosine = cosine * square + (-1) ** n * (2 * math.pi) ** (2 * n) / math.factorial(2 * n)
        sine = sine * square + (-1) ** n * (2 * math.pi) ** (2 * n + 1) / math.factorial(2 * n + 1)
    return cosine, sine * turn


def rows_iota(shape):
    return lax.broadcasted_iota(jnp.int32, shape, len(shape) - 2)


def lanes_iota(shape):
    return lax.broadcasted_iota(jnp.int32, shape, len(shape) - 1)


def pack_places(out_ref, places_ref, exports_ref, counts_ref, side):
    base = NH * BA
    out_ref[base : base + 8, :] = jnp.zeros((8, out_ref.shape[1]), f32)
    for s in range(NH):
        chosen = exports_ref[0, side, s]
        lane = side * base + s * BA
        found = places_ref[:, :BA]
        for b in range(1, NB):
            found = jnp.where(chosen == b, places_ref[:, b * BA : (b + 1) * BA], found)
        out_ref[base : base + 3, lane : lane + BA] = found
        live = jnp.where(s < counts_ref[0, side], 1.0, 0.0)
        out_ref[base + 3 : base + 4, lane : lane + BA] = jnp.full((1, BA), live, f32)


def pack_rows(out_ref, rows_ref, exports_ref, side):
    for s in range(NH):
        start = pl.multiple_of(exports_ref[0, side, s] * BA, BA)
        out_ref[s * BA : (s + 1) * BA, :] = rows_ref[pl.ds(start, BA), :]


def head_kernel(
    features_ref, places_ref, charge_ref, anchor_ref, exports_ref, counts_ref,
    up_ref, down_ref, payload_ref,
    staged,
):
    for out_ref, side in ((up_ref, 0), (down_ref, 1)):
        pack_rows(out_ref, features_ref, exports_ref, side)
        pack_places(out_ref, places_ref, exports_ref, counts_ref, side)
    width = charge_ref.shape[0]
    charge_rows = jnp.transpose(
        jnp.concatenate([charge_ref[...], jnp.zeros((width, 6), f32)], axis=1)
    )
    charges = product(split(charge_rows), split(features_ref[...]), NT)
    chunks = features_ref.shape[0] // LANES
    for t in range(chunks):
        lane = slice(t * LANES, (t + 1) * LANES)
        for c in range(2):
            staged[c * chunks + t : c * chunks + t + 1, :] = charges[c : c + 1, lane]
        for d in range(3):
            row = (2 + d) * chunks + t
            staged[row : row + 1, :] = places_ref[d : d + 1, lane]
    anchors = anchor_ref[...].astype(f32)
    block = lanes_iota((3, LANES)) % (NB * BZ) // BZ
    spread = jnp.broadcast_to(anchors[:, :1], (3, LANES))
    for b in range(1, NB):
        spread = jnp.where(block == b, anchors[:, b : b + 1], spread)
    staged[5 * chunks : 5 * chunks + 3, :] = spread
    lane = lanes_iota((1, LANES))
    listed = jnp.zeros((1, LANES), jnp.int32)
    for side in range(2):
        for s in range(NH):
            listed = jnp.where(lane == side * NH + s, exports_ref[0, side, s], listed)
    staged[5 * chunks + 3 :, :] = listed.astype(f32)
    payload = staged[...]

    @pl.loop(0, payload_ref.shape[0])
    def _(domain):
        payload_ref[domain] = payload


def pair_terms(squared, live):
    softened = squared + soften
    near = jnp.exp(-2.0 * softened)
    if live is not None:
        near = near * live
    return near, jnp.exp(STEP * jnp.sqrt(softened))


def squared_distance(columns, rows):
    total = None
    for d in range(3):
        delta = columns[:, d : d + 1] - rows[d : d + 1, :]
        total = delta * delta if total is None else total + delta * delta
    return total


def all_messages(values_ref, ghost_values_ref, places_ref, ghost_places, weight_ref, out_ref):
    weights = [weight_ref[k : k + 1, :] * float(FACTORS[k]) for k in range(NR)]
    atoms = values_ref.shape[0]
    columns = jnp.transpose(
        jnp.concatenate([places_ref[...], jnp.zeros((5, atoms), f32)], axis=0)
    )
    ghosts = 2 * NH * BA
    near, ratio = pair_terms(
        squared_distance(columns, ghost_places[:, :ghosts]), ghost_places[3:4, :ghosts]
    )
    ghost_values = ghost_values_ref[...]
    total = None
    term = near
    for k in range(0, NR, 2):
        after = term * ratio
        left = split(jnp.concatenate([term, after], axis=1))
        right = split(
            jnp.concatenate(
                [ghost_values * weights[k], ghost_values * weights[k + 1]],
                axis=0,
            )
        )
        part = product(left, right)
        total = part if total is None else total + part
        term = after * ratio
    out_ref[...] = total
    half = lanes_iota((BA, 2 * BA)) >= BA
    partner = lanes_iota((BA, 2 * BA)) % BA
    other = (partner != rows_iota((BA, 2 * BA))).astype(f32)
    for b in range(atoms // BA):
        rows = slice(b * BA, (b + 1) * BA)
        here = places_ref[:, rows]
        near, ratio = pair_terms(
            squared_distance(columns[rows], jnp.concatenate([here, here], axis=1)), other
        )
        term = jnp.where(half, near * ratio, near)
        ratio = ratio * ratio
        lefts, rights = [], []
        values = values_ref[rows, :]
        for k in range(0, NR, 2):
            lefts.append(term)
            rights.append(values * weights[k])
            rights.append(values * weights[k + 1])
            term = term * ratio
        out_ref[rows, :] += product(
            split(jnp.concatenate(lefts, axis=1)), split(jnp.concatenate(rights, axis=0))
        )


def finish(hidden, messages, output_ref):
    scaled = messages * lax.rsqrt(
        jnp.mean(messages * messages, axis=-1, keepdims=True) + norm_epsilon
    )
    active = scaled / (1.0 + jnp.exp(-scaled))
    return hidden + product(split(active), split(output_ref[...]))


def first_layer_kernel(
    features_ref, up_ref, down_ref, places_ref, value_one_ref, output_one_ref, weight_ref,
    value_two_ref, exports_ref,
    hidden_ref, values_two_ref, up_two_ref, down_two_ref, ghost_places_ref,
    values, ghost_values, messages,
):
    base = NH * BA
    value_weight = split(value_one_ref[...])
    values[...] = product(split(features_ref[...]), value_weight)
    ghost_values[:base, :] = product(split(up_ref[:base, :]), value_weight)
    ghost_values[base:, :] = product(split(down_ref[:base, :]), value_weight)
    ghost_places_ref[...] = up_ref[base : base + 8, :] + down_ref[base : base + 8, :]
    ghost_places = ghost_places_ref[...]
    all_messages(values, ghost_values, places_ref, ghost_places, weight_ref, messages)
    hidden_ref[...] = finish(features_ref[...], messages[...], output_one_ref)
    values_two_ref[...] = product(split(hidden_ref[...]), split(value_two_ref[...]))
    pack_rows(up_two_ref, values_two_ref, exports_ref, 0)
    pack_rows(down_two_ref, values_two_ref, exports_ref, 1)


def second_layer_kernel(
    values_ref, up_two_ref, down_two_ref, ghost_places_ref, places_ref, weight_ref,
    return_ref, value_two_ref,
    messages_ref, returned_ref,
    ghost_values,
):
    base = NH * BA
    ghost_values[:base, :] = up_two_ref[...]
    ghost_values[base:, :] = down_two_ref[...]
    ghost_places = ghost_places_ref[...]
    all_messages(values_ref, ghost_values, places_ref, ghost_places, weight_ref, messages_ref)
    return_rows = jnp.concatenate(
        [return_ref[...], jnp.zeros((6, return_ref.shape[1]), f32)], axis=0
    )
    returned_ref[...] = product(split(return_rows), split(value_two_ref[...]))


def tail_kernel(
    received_ref, messages_ref, hidden_ref, ghost_places_ref, places_ref, weight_ref,
    return_ref, returned_ref, output_two_ref,
    updated_ref,
):
    atoms = hidden_ref.shape[0]
    ghosts = 2 * NH * BA
    potentials = jnp.sum(received_ref[...], axis=0)
    columns = jnp.transpose(potentials)
    ghost_places = ghost_places_ref[...]
    ghost_columns = jnp.transpose(ghost_places[:, :ghosts])
    own_columns = jnp.transpose(
        jnp.concatenate([places_ref[...], jnp.zeros((5, atoms), f32)], axis=0)
    )
    half = lanes_iota((BA, LANES)) >= BA
    other = (lanes_iota((BA, LANES)) % BA != rows_iota((BA, LANES))).astype(f32)
    ghost_potential = [
        jnp.concatenate([columns[c * BA : (c + 1) * BA, NB + s : NB + s + 1] for s in range(2 * NH)], axis=0)
        for c in range(2)
    ]
    pieces = []
    for t in range(atoms // LANES):
        lane = slice(t * LANES, (t + 1) * LANES)
        here = places_ref[:, lane]
        near, ratio = pair_terms(squared_distance(ghost_columns, here), ghost_columns[:, 3:4])
        squared = None
        own_potential = []
        for c in range(2):
            own_potential.append(
                jnp.where(
                    half,
                    columns[c * BA : (c + 1) * BA, 2 * t + 1 : 2 * t + 2],
                    columns[c * BA : (c + 1) * BA, 2 * t : 2 * t + 1],
                )
            )
        for d in range(3):
            first = own_columns[2 * t * BA : (2 * t + 1) * BA, d : d + 1]
            second = own_columns[(2 * t + 1) * BA : (2 * t + 2) * BA, d : d + 1]
            delta = jnp.where(half, second, first) - here[d : d + 1, :]
            squared = delta * delta if squared is None else squared + delta * delta
        own_near, own_ratio = pair_terms(squared, other)
        ratio = jnp.concatenate([ratio, own_ratio], axis=0)
        terms = [
            jnp.concatenate([near * ghost_potential[c], own_near * own_potential[c]], axis=0)
            for c in range(2)
        ]
        sums = []
        for k in range(NR):
            for c in range(2):
                sums.append(jnp.sum(terms[c], axis=0, keepdims=True))
                if k + 1 < NR:
                    terms[c] = terms[c] * ratio
        pieces.append(jnp.concatenate(sums, axis=0))
    gathered = jnp.transpose(jnp.concatenate(pieces, axis=1))
    spread = jnp.concatenate(
        [
            returned_ref[c : c + 1, :] * (weight_ref[k : k + 1, :] * float(FACTORS[k]))
            for k in range(NR)
            for c in range(2)
        ],
        axis=0,
    )
    messages = messages_ref[...] + product(split(gathered), split(spread))
    back = [return_ref[c : c + 1, :] for c in range(2)]
    layer_input = jnp.concatenate(
        [
            hidden_ref[b * BA : (b + 1) * BA, :]
            + columns[:BA, b : b + 1] * back[0]
            + columns[BA:, b : b + 1] * back[1]
            for b in range(atoms // BA)
        ],
        axis=0,
    )
    updated_ref[...] = finish(layer_input, messages, output_two_ref)


def transform_tables(grid):
    half = grid // 2
    u = np.arange(grid)
    x = np.concatenate([np.arange(half + 1), np.arange(1, half)])
    angle = 2.0 * np.pi * (np.outer(u, x) % grid) / grid
    table = np.where(np.arange(grid)[None] <= half, np.cos(angle), np.sin(angle)).astype(np.float32)
    back = (table.T / float(grid) ** 3).astype(np.float32)
    return table, back


def reciprocal_kernel(
    grid, slabs, per_slab, second, depth,
    place_ref, exports_ref, payload_ref, green_ref, forward_ref, back_ref,
    out_ref,
    planes, turns_high, turns_low, spread_high, spread_low, brick, carry,
    shift_cos, shift_sin, stage_cos, stage_sin, chosen, potential,
):
    domains = slabs * per_slab
    half = grid // 2
    thick = grid // slabs
    starts = thick - BX + 1
    rows = 2 * second
    cells = per_slab * NB * BZ
    atoms = per_slab * NB * BA
    chunks = atoms // LANES
    own = NB * BA // LANES
    wide = depth
    first_v = (place_ref[0] * second).astype(f32)
    first_w = (place_ref[1] * place_ref[2]).astype(f32)
    period = float(grid)

    row = rows_iota((rows, 1))
    frequency = jnp.where(row >= second, row - second, row).astype(f32) + first_v
    cosine, sine = wave(jnp.broadcast_to(frequency, (rows, LANES)), period)
    shift_cos[...] = cosine
    shift_sin[...] = sine
    upper = rows_iota((rows, LANES)) >= second
    spread_high[...] = jnp.zeros(spread_high.shape, bf16)
    spread_low[...] = jnp.zeros(spread_low.shape, bf16)
    carry[...] = jnp.zeros(carry.shape, f32)
    left_half = lanes_iota((1, LANES)) < LANES // 2

    def atom_rows(slab, t):
        base = slab * per_slab + t // own
        return [payload_ref[base, q * own + t % own : q * own + t % own + 1, :] for q in range(5)]

    def windows(parts):
        cell = rows_iota((BY, LANES)).astype(f32)
        along_x = [jnp.exp(-((float(i) - parts[2] * 1.5) ** 2)) for i in range(BX)]
        along_y = jnp.exp(-((cell - parts[3] * 3.5) ** 2))
        along_z = jnp.exp(-((cell - parts[4] * 3.5) ** 2))
        return along_x, along_y, along_z

    def anchor(slab, dim):
        found = []
        for q in range(0, per_slab, 2):
            one = payload_ref[slab * per_slab + q, 5 * own + dim : 5 * own + dim + 1, :]
            two = payload_ref[slab * per_slab + q + 1, 5 * own + dim : 5 * own + dim + 1, :]
            found.append(jnp.where(left_half, one, two))
        return jnp.concatenate(found, axis=1) if len(found) > 1 else found[0]

    def fill_spread(slab):
        both = []
        for t in range(chunks):
            parts = atom_rows(slab, t)
            along = windows(parts)
            along_z = along[2]
            masked = jnp.concatenate(
                [jnp.where(left_half, along_z, 0.0), jnp.where(left_half, 0.0, along_z)], axis=0
            )
            high, low = split(masked)
            spread_high[t * 16 : (t + 1) * 16, t * LANES : (t + 1) * LANES] = high
            spread_low[t * 16 : (t + 1) * 16, t * LANES : (t + 1) * LANES] = low
            both.append((parts, along))
        return both

    def slab_masks(slab):
        start = anchor(slab, 0) - (slab * thick).astype(f32)
        return [(start == float(s)).astype(f32) for s in range(starts)]

    def deposit(slab):
        both = fill_spread(slab)
        lefts = []
        for parts, (along_x, along_y, _) in both:
            lefts.append(
                jnp.concatenate(
                    [(parts[c] * along_x[i]) * along_y for c in range(2) for i in range(BX)], axis=0
                )
            )
        brick[...] = product(
            split(jnp.concatenate(lefts, axis=1)), (spread_high[...], spread_low[...]), NT
        )
        low_cell = anchor(slab, 2) + (lanes_iota((1, cells)) % BZ).astype(f32)
        ramp = rows_iota((8, cells)).astype(f32) + first_w
        cosine, sine = wave(ramp * low_cell, period)
        turn_cos, turn_sin = wave(8.0 * low_cell, period)
        for g in range(wide // 8):
            at = slice(g * 8, (g + 1) * 8)
            stage_cos[at, :] = cosine
            stage_sin[at, :] = sine
            cosine, sine = cosine * turn_cos - sine * turn_sin, cosine * turn_sin + sine * turn_cos
        cos_high, cos_low = split(stage_cos[...])
        sin_high, sin_low = split(stage_sin[...])
        for ref, c_part, s_part in ((turns_high, cos_high, sin_high), (turns_low, cos_low, sin_low)):
            ref[slab, :wide, :cells] = c_part
            ref[slab, :wide, cells:] = s_part
            ref[slab, wide:, :cells] = -s_part
            ref[slab, wide:, cells:] = c_part
        wide_cos = jnp.concatenate([shift_cos[...]] * (cells // LANES), axis=1)
        wide_sin = jnp.concatenate([shift_sin[...]] * (cells // LANES), axis=1)
        top = jnp.concatenate([upper] * (cells // LANES), axis=1) if cells > LANES else upper
        cosine, sine = wave(frequency * anchor(slab, 1), period)
        real = [jnp.zeros((rows, cells), f32)] * BX
        imag = [jnp.zeros((rows, cells), f32)] * BX
        for j in range(BY):
            for i in range(BX):
                low = brick[i * BY + j : i * BY + j + 1, :]
                high = brick[(BX + i) * BY + j : (BX + i) * BY + j + 1, :]
                weight = jnp.where(top, high, low)
                real[i] = real[i] + weight * cosine
                imag[i] = imag[i] - weight * sine
            if j + 1 < BY:
                cosine, sine = (
                    cosine * wide_cos - sine * wide_sin,
                    cosine * wide_sin + sine * wide_cos,
                )
        masks = slab_masks(slab)
        placed = []
        for x in range(thick):
            parts = []
            for source in (real, imag):
                total = None
                for i in range(BX):
                    if 0 <= x - i < starts:
                        piece = source[i] * masks[x - i]
                        total = piece if total is None else total + piece
                parts.append(total)
            placed.append(jnp.concatenate(parts, axis=1))
        return product(
            split(jnp.concatenate(placed, axis=0)), (turns_high[slab], turns_low[slab]), NT
        )

    def put(x, value):
        planes[:, pl.ds(x, 1), :] = value[:, None, :]

    def get(x):
        return planes[:, pl.ds(x, 1), :][:, 0, :]

    def swapped(value):
        return jnp.concatenate([value[:, wide:], -value[:, :wide]], axis=1)

    @pl.loop(0, slabs // 2)
    def _(m):
        near = deposit(m)
        far = deposit(slabs - 1 - m)
        for r in range(thick):
            x = m * thick + r
            one = near[r * rows : (r + 1) * rows]
            if r == 0:
                two = carry[...]
            else:
                two = far[(thick - r) * rows : (thick - r + 1) * rows]
            put(x, one + two)
            put(half + x, swapped(one - two))
        carry[...] = far[:rows]

    put(half, carry[...])

    def padded(kernel):
        gap = wide - kernel.shape[1]
        if gap == 0:
            return kernel
        return jnp.concatenate([kernel, jnp.zeros((kernel.shape[0], gap), f32)], axis=1)

    table = split(forward_ref[...])
    table_back = split(back_ref[...])

    @pl.loop(0, second)
    def _(v):
        inside = jnp.concatenate([planes[v], planes[second + v]], axis=1)
        spectrum = product(table, split(inside))
        outside = []
        for c in range(2):
            zero, one = padded(green_ref[v, c, 0]), padded(green_ref[v, c, 1])
            for part in range(2):
                outside.append(
                    zero * spectrum[:, part * wide : (part + 1) * wide]
                    + one * spectrum[:, (2 + part) * wide : (3 + part) * wide]
                )
        result = product(table_back, split(jnp.concatenate(outside, axis=1)))
        planes[v] = result[:, : 2 * wide]
        planes[second + v] = result[:, 2 * wide :]

    def evaluate(slab, inputs):
        masks = slab_masks(slab)
        both = fill_spread(slab)
        found = product(
            split(jnp.concatenate(inputs, axis=0)), (turns_high[slab], turns_low[slab])
        )
        twice = [jnp.concatenate([mask, mask], axis=1) for mask in masks]
        for i in range(BX):
            total = None
            for s in range(starts):
                piece = found[(s + i) * rows : (s + i + 1) * rows] * twice[s]
                total = piece if total is None else total + piece
            chosen[i * rows : (i + 1) * rows, :] = total
        cell = anchor(slab, 1) + rows_iota((BY, cells)).astype(f32)
        cosine, sine = wave(cell * first_v, period)
        turn_cos, turn_sin = wave(cell, period)
        sums = [jnp.zeros((BY, cells), f32)] * (2 * BX)
        for v in range(second):
            for c in range(2):
                for i in range(BX):
                    at = i * rows + c * second + v
                    sums[c * BX + i] = (
                        sums[c * BX + i]
                        + chosen[at : at + 1, :cells] * cosine
                        - chosen[at : at + 1, cells:] * sine
                    )
            if v + 1 < second:
                cosine, sine = cosine * turn_cos - sine * turn_sin, cosine * turn_sin + sine * turn_cos
        at_atoms = product(
            split(jnp.concatenate(sums, axis=0)), (spread_high[...], spread_low[...])
        )
        for t in range(chunks):
            lane = slice(t * LANES, (t + 1) * LANES)
            _, (along_x, along_y, _) = both[t]
            pair = []
            for c in range(2):
                total = None
                for i in range(BX):
                    at = (c * BX + i) * BY
                    piece = at_atoms[at : at + BY, lane] * along_x[i]
                    total = piece if total is None else total + piece
                pair.append(jnp.sum(total * along_y, axis=0, keepdims=True))
            one = jnp.where(left_half, pair[0], pltpu.roll(pair[1], LANES // 2, 1))
            two = jnp.where(left_half, pltpu.roll(pair[0], LANES // 2, 1), pair[1])
            potential[pl.ds(slab * per_slab * NB + 2 * t, 1), :] = one
            potential[pl.ds(slab * per_slab * NB + 2 * t + 1, 1), :] = two

    def straight(x):
        even = get(x)
        odd = get(jnp.minimum(half + x, grid - 1)) * jnp.where((x > 0) & (x < half), 1.0, 0.0)
        turned = jnp.concatenate([-odd[:, wide:], odd[:, :wide]], axis=1)
        return even + turned, even - turned

    @pl.loop(0, slabs // 2)
    def _(m):
        near, far = [], [None] * thick
        for r in range(thick):
            ahead, behind = straight(m * thick + r)
            near.append(ahead)
            if r > 0:
                far[thick - r] = behind
        far[0] = straight(m * thick + thick)[1]
        evaluate(m, near)
        evaluate(slabs - 1 - m, far)

    @pl.loop(0, domains)
    def _(domain):
        out_ref[domain, NB + 2 * NH :, :] = jnp.zeros((16 - NB - 2 * NH, LANES), f32)
        out_ref[domain, :NB, :] = potential[pl.ds(pl.multiple_of(domain * NB, NB), NB), :]
        below = lax.rem(domain + domains - 1, domains)
        above = lax.rem(domain + 1, domains)
        for s in range(NH):
            at = below * NB + exports_ref[below, s]
            out_ref[domain, NB + s : NB + s + 1, :] = potential[pl.ds(at, 1), :]
            at = above * NB + exports_ref[above, NH + s]
            out_ref[domain, NB + NH + s : NB + NH + s + 1, :] = potential[pl.ds(at, 1), :]


def build_reciprocal(grid, slabs, per_slab, second, depth):
    domains = slabs * per_slab
    cells = per_slab * NB * BZ
    slab_atoms = per_slab * NB * BA
    return pl.pallas_call(
        functools.partial(reciprocal_kernel, grid, slabs, per_slab, second, depth),
        in_specs=[SMEM, SMEM] + [VMEM] * 4,
        out_specs=VMEM,
        out_shape=jax.ShapeDtypeStruct((domains, 16, LANES), f32),
        scratch_shapes=[
            pltpu.VMEM((2 * second, grid, 2 * depth), f32),
            pltpu.VMEM((slabs, 2 * depth, 2 * cells), bf16),
            pltpu.VMEM((slabs, 2 * depth, 2 * cells), bf16),
            pltpu.VMEM((cells, slab_atoms), bf16),
            pltpu.VMEM((cells, slab_atoms), bf16),
            pltpu.VMEM((2 * BX * BY, cells), f32),
            pltpu.VMEM((2 * second, 2 * depth), f32),
            pltpu.VMEM((2 * second, LANES), f32),
            pltpu.VMEM((2 * second, LANES), f32),
            pltpu.VMEM((depth, cells), f32),
            pltpu.VMEM((depth, cells), f32),
            pltpu.VMEM((BX * 2 * second, 2 * cells), f32),
            pltpu.VMEM((domains * NB, LANES), f32),
        ],
        compiler_params=params(),
    )


VMEM = pl.BlockSpec(memory_space=pltpu.VMEM)
SMEM = pl.BlockSpec(memory_space=pltpu.SMEM)


def per_device(
    features,
    positions,
    value_one,
    output_one,
    radial_one,
    value_two,
    output_two,
    radial_two,
    charge_weight,
    return_weight,
    green_kernel,
    exports,
    export_counts,
    brick_anchor,
):
    axes = ("dom", "rec")
    slabs, per_slab = lax.axis_size("dom"), lax.axis_size("rec")
    domains = slabs * per_slab
    atoms, width = features.shape
    depth_rows, grid, second = green_kernel.shape[0], green_kernel.shape[3], green_kernel.shape[4]
    depth = -(-depth_rows // LANES) * LANES
    chunks = atoms // LANES
    payload_rows = 5 * chunks + 4
    base = NH * BA

    def shape(*dims):
        return jax.ShapeDtypeStruct(dims, f32)

    def around(rows, by):
        return lax.ppermute(rows, axes, [(i, (i + by) % domains) for i in range(domains)])

    up, down, payload = pl.pallas_call(
        head_kernel,
        in_specs=[VMEM] * 4 + [SMEM] * 2,
        out_specs=[VMEM] * 3,
        out_shape=[
            shape(base + 8, width), shape(base + 8, width), shape(domains, payload_rows, LANES)
        ],
        scratch_shapes=[pltpu.VMEM((payload_rows, LANES), f32)],
        compiler_params=params(),
    )(features, positions, charge_weight, brick_anchor, exports, export_counts)

    up, down, green_kernel = lax.optimization_barrier((up, down, green_kernel))
    green = jnp.transpose(green_kernel, (4, 1, 2, 3, 0))
    up = around(up, 1)
    down = around(down, -1)
    payload, green, up, down = lax.optimization_barrier((payload, green, up, down))
    everyone = lax.all_to_all(payload, axes, 0, 0, tiled=True)

    hidden, values_two, up_two, down_two, ghost_places = pl.pallas_call(
        first_layer_kernel,
        in_specs=[VMEM] * 8 + [SMEM],
        out_specs=[VMEM] * 5,
        out_shape=[
            shape(atoms, width), shape(atoms, width), shape(base, width), shape(base, width),
            shape(8, width),
        ],
        scratch_shapes=[
            pltpu.VMEM((atoms, width), f32),
            pltpu.VMEM((2 * base, width), f32),
            pltpu.VMEM((atoms, width), f32),
        ],
        compiler_params=params(),
    )(features, up, down, positions, value_one, output_one, radial_one, value_two, exports)

    everyone, hidden = lax.optimization_barrier((everyone, hidden))
    up_two = around(up_two, 1)
    down_two = around(down_two, -1)

    place = jnp.stack(
        [lax.axis_index("dom"), lax.axis_index("rec"), jnp.int32(depth_rows)]
    ).astype(jnp.int32)
    all_exports = everyone[:, 5 * chunks + 3, :8].astype(jnp.int32)
    table, table_back = transform_tables(grid)
    outgoing = build_reciprocal(grid, slabs, per_slab, second, depth)(
        place, all_exports, everyone, green, table, table_back
    )

    outgoing, up_two, down_two = lax.optimization_barrier((outgoing, up_two, down_two))
    received = lax.all_to_all(outgoing, axes, 0, 0, tiled=True)

    messages, returned = pl.pallas_call(
        second_layer_kernel,
        in_specs=[VMEM] * 8,
        out_specs=[VMEM] * 2,
        out_shape=[shape(atoms, width), shape(8, width)],
        scratch_shapes=[pltpu.VMEM((2 * base, width), f32)],
        compiler_params=params(),
    )(values_two, up_two, down_two, ghost_places, positions, radial_two, return_weight, value_two)

    return pl.pallas_call(
        tail_kernel,
        in_specs=[VMEM] * 9,
        out_specs=VMEM,
        out_shape=shape(atoms, width),
        compiler_params=params(),
    )(
        received, messages, hidden, ghost_places, positions, radial_two, return_weight, returned, output_two
    )


def solution(mesh):
    placed = (
        P(("dom", "rec"), None),
        P(None, ("dom", "rec")),
        P(),
        P(),
        P(),
        P(),
        P(),
        P(),
        P(),
        P(),
        P("rec", None, None, None, "dom"),
        P(("dom", "rec"), None, None),
        P(("dom", "rec"), None),
        P(None, ("dom", "rec")),
    )
    return jax.shard_map(
        per_device, mesh=mesh, in_specs=placed, out_specs=P(("dom", "rec"), None), check_vma=False
    )
```

time: 847 us -> 120 us (0.14); the launches traced: 836 us -> 119 us
  blocking collectives: 218 us -> 0 us
  waiting for transfers between devices: 195 us -> 7.24 us
  matrix products: 172 us -> 0 us
  local copies, waits for them, and re-layouts: 131 us -> 10.1 us
  Pallas kernels: 0 us -> 80.4 us
  other arithmetic: 46.1 us -> 1.34 us
  loops' own time: 36.8 us -> 0 us
  between operations: 14.3 us -> 0.08 us
    all_to_all x2 -> x0, blocking collectives: 218 us -> none  [the longest x1 109 us: reciprocal(): lax.all_to_all(jnp.stack([second_real, second_imag], axis=1), 'dom', spli...]
    dot_general x30 -> x0, matrix products: 172 us -> none  [the longest x2 32 us: block_messages(): jnp.einsum('kbip,bpf->kbif', radial_terms, partner_values, precision=exac...]
    reduce_scatter x1 -> x0, waiting for transfers between devices: 114 us -> none  [reciprocal(): lax.psum_scatter(jnp.stack([real_part, imag_part], axis=1), 'rec', scatte...]
    pallas_call x0 -> x5, Pallas kernels: none -> 80.4 us  [the longest x1 43 us: per_device(): build_reciprocal(grid, slabs, per_slab, second, depth)]
    all_gather x1 -> x0, waiting for transfers between devices: 62.2 us -> none  [reciprocal(): piece = lax.all_gather(planes, 'rec', axis=0, tiled=True)]
    gather x35 -> x0, local copies, waits for them, and re-layouts: 38.3 us -> none
    another operation x2 -> x0, loops' own time: 36.8 us -> none  [the longest x1 36.6 us: reciprocal(): lax.fori_loop(0, blocks, deposit, jnp.zeros((2, slab_depth, grid_size, gr...]
    dynamic_update_slice x8 -> x0, local copies, waits for them, and re-layouts: 30.5 us -> none  [deposit(): lax.dynamic_update_slice(slab, lax.dynamic_slice(slab, corner, (2, BX, BY...]
  transfers between devices with their start and end apart: 10 -> 6, of which waited for: 6 -> 2; matrix products, arithmetic and copies ran while one was open for 5% -> 8% of each run, Pallas kernels for 0% -> 59%
where the time goes in v1:
time: 120 us; the launch traced here: 119 us
  Pallas kernels  80.4 us (67%)
  starting transfers between devices  20.2 us (17%)
  local copies, waits for them, and re-layouts  10.1 us (8%)
  waiting for transfers between devices  7.24 us (6%)
  other arithmetic  1.34 us (1%)
    pallas_call x1, Pallas kernels, per_device(): build_reciprocal(grid, slabs, per_slab, second, depth)  43 us
    pallas_call x1, Pallas kernels, per_device(): pl.pallas_call(first_layer_kernel, in_specs=[VMEM] * 8 + [SMEM], out_spec...  15.4 us
    ppermute x4, starting transfers between devices, around(): lax.ppermute(rows, axes, [(i, (i + by) % domains) for i in range(domains)])  11.8 us
    pallas_call x1, Pallas kernels, per_device(): pl.pallas_call(second_layer_kernel, in_specs=[VMEM] * 8, out_specs=[VMEM]...  11.5 us
    optimization_barrier x1, local copies, waits for them, and re-layouts, per_device(): up, down, green_kernel = lax.optimization_barrier((up, down, green_kernel))  7.73 us
    pallas_call x1, Pallas kernels, per_device(): pl.pallas_call(tail_kernel, in_specs=[VMEM] * 9, out_specs=VMEM, out_shap...  7.29 us
    ppermute x4, waiting for transfers between devices, around(): lax.ppermute(rows, axes, [(i, (i + by) % domains) for i in range(domains)])  7.24 us
    all_to_all x1, starting transfers between devices, per_device(): everyone = lax.all_to_all(payload, axes, 0, 0, tiled=True)  5.82 us
  transfers between devices with their start and end apart: 6, of which 2 were waited for; matrix products, arithmetic and copies ran while one was open for 8% of the time, Pallas kernels for 59%

profile of v1, /device:TPU:0, one launch (start us, length us, event | category | flops | bytes accessed | tf_op | source)
XLA Modules:
  0.0 119.4 jit_solution(14567009496887037188)
XLA Ops:
  0.0 1.6 %copy.17.charge_ref = f32[512,2]{1,0:T(8,128)} copy(f32[512,2]{0,1:T(2,128)} %param.24) | data formatting | bytes 8192 | tf_op args[8]
  1.6 3.2 %shard_map.154 = (f32[200,512]{1,0:T(8,128)}, f32[200,512]{1,0:T(8,128)}, f32[32,24,128]{2,1,0:T(8,128)}) custom-call(f32[512,512]{1,0:T(8,128)} %features_ref.3, f32[3,512]{1,0:T(4,128)} %places_ref.7, f32[512,2]{1,0:T(8,128)} %copy.17.charge_ref, s32[3,8]{1,0:T(4,128)} %anchor_ref.1, s32[1,2,3]{2,1,0:T(2,128)} %exports_ref.3, s32[1,2]{1,0:T(1,128)} %counts_ref.1), custom_call_target="tpu_custom_call" | custom-call | tf_op jit(solution)/shard_map/pallas_call | solution.py:648
  4.7 2.9 %collective-permute-start = (f32[200,512]{1,0:T(8,128)}, f32[200,512]{1,0:T(8,128)S(1)}, u32[]{:S(2)}, u32[]{:S(2)}) collective-permute-start(f32[200,512]{1,0:T(8,128)} %get-tuple-element.31), channel_id=1, source_target_pairs={{0,1},{1,2},{2,3},{3,4},{4,5},{5,6},{6,7},{7,8},{8,9},{9,10},{10,1... | collective-permute-start | bytes 1228808 | tf_op jit(solution)/shard_map/ppermute | solution.py:646
  7.7 3.4 %collective-permute-start.1 = (f32[200,512]{1,0:T(8,128)}, f32[200,512]{1,0:T(8,128)S(1)}, u32[]{:S(2)}, u32[]{:S(2)}) collective-permute-start(f32[200,512]{1,0:T(8,128)} %get-tuple-element.32), channel_id=1, source_target_pairs={{0,31},{1,0},{2,1},{3,2},{4,3},{5,4},{6,5},{7,6},{8,7},{9,8},{10,9... | collective-permute-start | bytes 1228808 | tf_op jit(solution)/shard_map/ppermute | solution.py:646
  11.1 7.7 %copy.18 = f32[96,2,2,192,12]{0,3,2,1,4:T(8,128)} copy(f32[96,2,2,192,12]{3,2,4,1,0:T(2,128)} %param.26) | data formatting | bytes 7077888 | tf_op jit(solution)/shard_map/optimization_barrier | solution.py:659
  18.8 3.4 %collective-permute-done.up_ref = f32[200,512]{1,0:T(8,128)S(1)} collective-permute-done((f32[200,512]{1,0:T(8,128)}, f32[200,512]{1,0:T(8,128)S(1)}, u32[]{:S(2)}, u32[]{:S(2)}) %collective-permute-start) | collective-permute-done | bytes 409632 | tf_op jit(solution)/shard_map/ppermute | solution.py:646
  22.2 0.0 copy-start.2
  22.2 3.8 %collective-permute-done.1.down_ref = f32[200,512]{1,0:T(8,128)S(1)} collective-permute-done((f32[200,512]{1,0:T(8,128)}, f32[200,512]{1,0:T(8,128)S(1)}, u32[]{:S(2)}, u32[]{:S(2)}) %collective-permute-start.1) | collective-permute-done | bytes 409632 | tf_op jit(solution)/shard_map/ppermute | solution.py:646
  26.1 0.0 copy-start.3
  26.1 5.8 %all-to-all-start = ((f32[32,24,128]{2,1,0:T(8,128)}), f32[32,24,128]{2,1,0:T(8,128)S(1)}, u32[]{:S(2)}, u32[]{:S(2)}) async-start(f32[32,24,128]{2,1,0:T(8,128)} %get-tuple-element.33), calls=%async_computation | async-start | bytes 786432 | tf_op jit(solution)/shard_map/all_to_all | solution.py:664
  31.9 0.0 copy-done.2
  31.9 0.0 copy-done.3
  31.9 15.4 %shard_map.155 = (f32[512,512]{1,0:T(8,128)}, f32[512,512]{1,0:T(8,128)}, f32[192,512]{1,0:T(8,128)}, f32[192,512]{1,0:T(8,128)}, f32[8,512]{1,0:T(8,128)}) custom-call(f32[512,512]{1,0:T(8,128)} %features_ref.3, f32[200,512]{1,0:T(8,128)} %copy-done.2, f32[200,512]{1,0:T(8,128)} %copy-done.3, f32[3,512]{1,0:T(4,128)} %places_ref.7, ...), custom_call_target="tpu_custom_call" | custom-call | tf_op jit(solution)/shard_map/pallas_call | solution.py:666
  47.4 1.7 %collective-permute-start.2 = (f32[192,512]{1,0:T(8,128)}, f32[192,512]{1,0:T(8,128)S(1)}, u32[]{:S(2)}, u32[]{:S(2)}) collective-permute-start(f32[192,512]{1,0:T(8,128)} %get-tuple-element.39), channel_id=1, source_target_pairs={{0,1},{1,2},{2,3},{3,4},{4,5},{5,6},{6,7},{7,8},{8,9},{9,10},{10,1... | collective-permute-start | bytes 1179656 | tf_op jit(solution)/shard_map/ppermute | solution.py:646
  49.1 3.7 %collective-permute-start.3 = (f32[192,512]{1,0:T(8,128)}, f32[192,512]{1,0:T(8,128)S(1)}, u32[]{:S(2)}, u32[]{:S(2)}) collective-permute-start(f32[192,512]{1,0:T(8,128)} %get-tuple-element.40), channel_id=1, source_target_pairs={{0,31},{1,0},{2,1},{3,2},{4,3},{5,4},{6,5},{7,6},{8,7},{9,8},{10,9... | collective-permute-start | bytes 1179656 | tf_op jit(solution)/shard_map/ppermute | solution.py:646
  52.8 0.6 pad_add_fusion.place_ref
  53.4 0.0 all-to-all-done.payload_ref
  53.4 0.0 copy-start
  53.4 0.7 slice_convert_fusion
  54.1 0.0 copy-done
  54.2 43.0 %shard_map.156 = f32[32,16,128]{2,1,0:T(8,128)} custom-call(s32[3]{0:T(128)} %pad_add_fusion.place_ref, s32[32,8]{1,0:T(8,128)} %bitcast.5, f32[32,24,128]{2,1,0:T(8,128)} %copy-done, f32[12,2,2,192,96]{4,3,2,1,0:T(8,128)} %bitcast.4, f32[192,192]{1,0:T(8,128)} %constant.14.clone.forward_ref, f32[192,192]{1,0:T(8,128)} %constant.15.clone.back_ref), custom_call_target="tpu_custom_call" | custom-call | tf_op jit(solution)/shard_map/pallas_call | solution.py:691
  97.2 0.0 collective-permute-done.2.up_two_ref
  97.2 0.0 copy-start.4
  97.2 0.0 collective-permute-done.3.down_two_ref
  97.2 0.0 copy-start.5
  97.2 2.6 %all-to-all-start.1 = ((f32[32,16,128]{2,1,0:T(8,128)}), f32[32,16,128]{2,1,0:T(8,128)S(1)}, u32[]{:S(2)}, u32[]{:S(2)}) async-start(f32[32,16,128]{2,1,0:T(8,128)} %shard_map.156), calls=%async_computation.1 | async-start | bytes 524288 | tf_op jit(solution)/shard_map/all_to_all | solution.py:696
  99.8 0.0 copy-done.4
  99.8 0.0 copy-done.5
  99.8 11.5 %shard_map.157 = (f32[512,512]{1,0:T(8,128)}, f32[8,512]{1,0:T(8,128)}) custom-call(f32[512,512]{1,0:T(8,128)} %get-tuple-element.42.values_ref, f32[192,512]{1,0:T(8,128)} %copy-done.4, f32[192,512]{1,0:T(8,128)} %copy-done.5, f32[8,512]{1,0:T(8,128)} %get-tuple-element.45.ghost_places_ref, f32[3,512]{1,0:T(4,128)} %places_ref.7, f32[8,512]{1,0:T(8,128)} %weight_ref.5, ...), custom_call_target="tpu_custom_call" | custom-call | tf_op jit(solution)/shard_map/pallas_call | solution.py:698
  111.4 0.0 all-to-all-done.1.received_ref
  111.4 0.0 copy-start.1
  111.4 0.7 copy-done.1
  112.1 7.3 %shard_map.158 = f32[512,512]{1,0:T(8,128)} custom-call(f32[32,16,128]{2,1,0:T(8,128)} %copy-done.1, f32[512,512]{1,0:T(8,128)} %get-tuple-element.46.messages_ref, f32[512,512]{1,0:T(8,128)} %get-tuple-element.47.hidden_ref, f32[8,512]{1,0:T(8,128)} %get-tuple-element.45.ghost_places_ref, f32[3,512]{1,0:T(4,128)} %places_ref.7, f32[8,512]{1,0:T(8,128)} %weight_ref.5, ...), custom_call_target="tpu_custom_call" | custom-call | tf_op jit(solution)/shard_map/pallas_call | solution.py:707
Async XLA Ops:
  4.7 17.5 %collective-permute-start = (f32[200,512]{1,0:T(8,128)}, f32[200,512]{1,0:T(8,128)S(1)}, u32[]{:S(2)}, u32[]{:S(2)}) collective-permute-start(f32[200,512]{1,0:T(8,128)} %get-tuple-element.31), channel_id=1, source_target_pairs={{0,1},{1,2},{2,3},{3,4},{4,5},{5,6},{6,7},{7,8},{8,9},{9,10},{10,1... | collective-permute-start | bytes 1228808 | tf_op jit(solution)/shard_map/ppermute | solution.py:646
  7.7 18.4 %collective-permute-start.1 = (f32[200,512]{1,0:T(8,128)}, f32[200,512]{1,0:T(8,128)S(1)}, u32[]{:S(2)}, u32[]{:S(2)}) collective-permute-start(f32[200,512]{1,0:T(8,128)} %get-tuple-element.32), channel_id=1, source_target_pairs={{0,31},{1,0},{2,1},{3,2},{4,3},{5,4},{6,5},{7,6},{8,7},{9,8},{10,9... | collective-permute-start | bytes 1228808 | tf_op jit(solution)/shard_map/ppermute | solution.py:646
  22.2 9.7 %copy-start.2 = (f32[200,512]{1,0:T(8,128)}, f32[200,512]{1,0:T(8,128)S(1)}, u32[]{:S(2)}) copy-start(f32[200,512]{1,0:T(8,128)S(1)} %collective-permute-done.up_ref) | copy-start | bytes 1228804
  26.1 5.8 %copy-start.3 = (f32[200,512]{1,0:T(8,128)}, f32[200,512]{1,0:T(8,128)S(1)}, u32[]{:S(2)}) copy-start(f32[200,512]{1,0:T(8,128)S(1)} %collective-permute-done.1.down_ref) | copy-start | bytes 1228804
  26.1 27.4 %all-to-all-start = ((f32[32,24,128]{2,1,0:T(8,128)}), f32[32,24,128]{2,1,0:T(8,128)S(1)}, u32[]{:S(2)}, u32[]{:S(2)}) async-start(f32[32,24,128]{2,1,0:T(8,128)} %get-tuple-element.33), calls=%async_computation | async-start | bytes 786432 | tf_op jit(solution)/shard_map/all_to_all | solution.py:664
  47.4 49.8 %collective-permute-start.2 = (f32[192,512]{1,0:T(8,128)}, f32[192,512]{1,0:T(8,128)S(1)}, u32[]{:S(2)}, u32[]{:S(2)}) collective-permute-start(f32[192,512]{1,0:T(8,128)} %get-tuple-element.39), channel_id=1, source_target_pairs={{0,1},{1,2},{2,3},{3,4},{4,5},{5,6},{6,7},{7,8},{8,9},{9,10},{10,1... | collective-permute-start | bytes 1179656 | tf_op jit(solution)/shard_map/ppermute | solution.py:646
  49.1 48.1 %collective-permute-start.3 = (f32[192,512]{1,0:T(8,128)}, f32[192,512]{1,0:T(8,128)S(1)}, u32[]{:S(2)}, u32[]{:S(2)}) collective-permute-start(f32[192,512]{1,0:T(8,128)} %get-tuple-element.40), channel_id=1, source_target_pairs={{0,31},{1,0},{2,1},{3,2},{4,3},{5,4},{6,5},{7,6},{8,7},{9,8},{10,9... | collective-permute-start | bytes 1179656 | tf_op jit(solution)/shard_map/ppermute | solution.py:646
  53.4 0.7 copy-start
  97.2 2.6 %copy-start.4 = (f32[192,512]{1,0:T(8,128)}, f32[192,512]{1,0:T(8,128)S(1)}, u32[]{:S(2)}) copy-start(f32[192,512]{1,0:T(8,128)S(1)} %collective-permute-done.2.up_two_ref) | copy-start | bytes 1179652
  97.2 2.6 %copy-start.5 = (f32[192,512]{1,0:T(8,128)}, f32[192,512]{1,0:T(8,128)S(1)}, u32[]{:S(2)}) copy-start(f32[192,512]{1,0:T(8,128)S(1)} %collective-permute-done.3.down_two_ref) | copy-start | bytes 1179652
  97.2 14.2 %all-to-all-start.1 = ((f32[32,16,128]{2,1,0:T(8,128)}), f32[32,16,128]{2,1,0:T(8,128)S(1)}, u32[]{:S(2)}, u32[]{:S(2)}) async-start(f32[32,16,128]{2,1,0:T(8,128)} %shard_map.156), calls=%async_computation.1 | async-start | bytes 524288 | tf_op jit(solution)/shard_map/all_to_all | solution.py:696
  111.4 0.7 copy-start.1

commit v2 on v1

--- a/solution.py
+++ b/solution.py
@@ -25,6 +25,7 @@
 NN = (((1,), (0,)), ((), ()))
 NT = (((1,), (1,)), ((), ()))
 STEP = 12.0 / 7.0
+OWN_GROUP = 4
 FACTORS = np.exp(-18.0 * np.arange(NR) ** 2 / 49.0).astype(np.float32)
 
 
@@ -38,8 +39,18 @@
 
 
 def product(left, right, dims=NN):
+    axis = dims[0][1][0]
+    return lax.dot_general(
+        jnp.concatenate([left[0], left[0], left[1]], axis=1),
+        jnp.concatenate([right[0], right[1], right[0]], axis=axis),
+        dims,
+        preferred_element_type=f32,
+    )
+
+
+def narrow_product(left, right):
     def one(a, b):
-        return lax.dot_general(a, b, dims, preferred_element_type=f32)
+        return lax.dot_general(a, b, NN, preferred_element_type=f32)
 
     return one(left[0], right[0]) + (one(left[0], right[1]) + one(left[1], right[0]))
 
@@ -62,6 +73,19 @@
 
 def lanes_iota(shape):
     return lax.broadcasted_iota(jnp.int32, shape, len(shape) - 1)
+
+
+def side_by_side(works):
+    results = [None] * len(works)
+    waiting = list(range(len(works)))
+    while waiting:
+        for n in list(waiting):
+            try:
+                next(works[n])
+            except StopIteration as end:
+                results[n] = end.value
+                waiting.remove(n)
+    return results
 
 
 def pack_places(out_ref, places_ref, exports_ref, counts_ref, side):
@@ -140,36 +164,52 @@
     return total
 
 
-def all_messages(values_ref, ghost_values_ref, places_ref, ghost_places, weight_ref, out_ref):
-    weights = [weight_ref[k : k + 1, :] * float(FACTORS[k]) for k in range(NR)]
-    atoms = values_ref.shape[0]
-    columns = jnp.transpose(
-        jnp.concatenate([places_ref[...], jnp.zeros((5, atoms), f32)], axis=0)
-    )
+def scaled_weights(weight_ref):
+    return [weight_ref[k : k + 1, :] * float(FACTORS[k]) for k in range(NR)]
+
+
+def place_columns(places_ref):
+    atoms = places_ref.shape[1]
+    return jnp.transpose(jnp.concatenate([places_ref[...], jnp.zeros((5, atoms), f32)], axis=0))
+
+
+def ghost_messages(ghost_values_ref, places_ref, ghost_places, weight_ref, out_ref):
+    weights = scaled_weights(weight_ref)
     ghosts = 2 * NH * BA
     near, ratio = pair_terms(
-        squared_distance(columns, ghost_places[:, :ghosts]), ghost_places[3:4, :ghosts]
-    )
-    ghost_values = ghost_values_ref[...]
-    total = None
+        squared_distance(place_columns(places_ref), ghost_places[:, :ghosts]),
+        ghost_places[3:4, :ghosts],
+    )
     term = near
-    for k in range(0, NR, 2):
+
+    def operands(k):
+        nonlocal term
         after = term * ratio
         left = split(jnp.concatenate([term, after], axis=1))
-        right = split(
-            jnp.concatenate(
-                [ghost_values * weights[k], ghost_values * weights[k + 1]],
-                axis=0,
-            )
+        term = after * ratio
+        values = ghost_values_ref[...]
+        return left, split(
+            jnp.concatenate([values * weights[k], values * weights[k + 1]], axis=0)
         )
-        part = product(left, right)
-        total = part if total is None else total + part
-        term = after * ratio
+
+    total = out_ref[...]
+    ready = operands(0)
+    for k in range(0, NR, 2):
+        following = operands(k + 2) if k + 2 < NR else None
+        total = total + product(*ready)
+        ready = following
     out_ref[...] = total
+
+
+def own_messages(values_ref, places_ref, weight_ref, out_ref):
+    weights = scaled_weights(weight_ref)
+    atoms = values_ref.shape[0]
+    columns = place_columns(places_ref)
     half = lanes_iota((BA, 2 * BA)) >= BA
     partner = lanes_iota((BA, 2 * BA)) % BA
     other = (partner != rows_iota((BA, 2 * BA))).astype(f32)
-    for b in range(atoms // BA):
+
+    def one_block(b):
         rows = slice(b * BA, (b + 1) * BA)
         here = places_ref[:, rows]
         near, ratio = pair_terms(
@@ -184,9 +224,14 @@
             rights.append(values * weights[k])
             rights.append(values * weights[k + 1])
             term = term * ratio
-        out_ref[rows, :] += product(
-            split(jnp.concatenate(lefts, axis=1)), split(jnp.concatenate(rights, axis=0))
-        )
+        left = split(jnp.concatenate(lefts, axis=1))
+        right = split(jnp.concatenate(rights, axis=0))
+        yield
+        out_ref[rows, :] = product(left, right)
+
+    blocks = atoms // BA
+    for b in range(0, blocks, OWN_GROUP):
+        side_by_side([one_block(b + n) for n in range(OWN_GROUP)])
 
 
 def finish(hidden, messages, output_ref):
@@ -197,20 +242,23 @@
     return hidden + product(split(active), split(output_ref[...]))
 
 
+def first_own_kernel(features_ref, places_ref, value_one_ref, weight_ref, messages_ref, values):
+    values[...] = product(split(features_ref[...]), split(value_one_ref[...]))
+    own_messages(values, places_ref, weight_ref, messages_ref)
+
+
 def first_layer_kernel(
-    features_ref, up_ref, down_ref, places_ref, value_one_ref, output_one_ref, weight_ref,
+    features_ref, own_ref, up_ref, down_ref, places_ref, value_one_ref, output_one_ref, weight_ref,
     value_two_ref, exports_ref,
     hidden_ref, values_two_ref, up_two_ref, down_two_ref, ghost_places_ref,
-    values, ghost_values, messages,
+    ghost_values, messages,
 ):
     base = NH * BA
-    value_weight = split(value_one_ref[...])
-    values[...] = product(split(features_ref[...]), value_weight)
-    ghost_values[:base, :] = product(split(up_ref[:base, :]), value_weight)
-    ghost_values[base:, :] = product(split(down_ref[:base, :]), value_weight)
+    ghost_rows = jnp.concatenate([up_ref[:base, :], down_ref[:base, :]], axis=0)
+    ghost_values[...] = product(split(ghost_rows), split(value_one_ref[...]))
     ghost_places_ref[...] = up_ref[base : base + 8, :] + down_ref[base : base + 8, :]
-    ghost_places = ghost_places_ref[...]
-    all_messages(values, ghost_values, places_ref, ghost_places, weight_ref, messages)
+    messages[...] = own_ref[...]
+    ghost_messages(ghost_values, places_ref, ghost_places_ref[...], weight_ref, messages)
     hidden_ref[...] = finish(features_ref[...], messages[...], output_one_ref)
     values_two_ref[...] = product(split(hidden_ref[...]), split(value_two_ref[...]))
     pack_rows(up_two_ref, values_two_ref, exports_ref, 0)
@@ -226,8 +274,8 @@
     base = NH * BA
     ghost_values[:base, :] = up_two_ref[...]
     ghost_values[base:, :] = down_two_ref[...]
-    ghost_places = ghost_places_ref[...]
-    all_messages(values_ref, ghost_values, places_ref, ghost_places, weight_ref, messages_ref)
+    own_messages(values_ref, places_ref, weight_ref, messages_ref)
+    ghost_messages(ghost_values, places_ref, ghost_places_ref[...], weight_ref, messages_ref)
     return_rows = jnp.concatenate(
         [return_ref[...], jnp.zeros((6, return_ref.shape[1]), f32)], axis=0
     )
@@ -296,7 +344,7 @@
         ],
         axis=0,
     )
-    messages = messages_ref[...] + product(split(gathered), split(spread))
+    messages = messages_ref[...] + narrow_product(split(gathered), split(spread))
     back = [return_ref[c : c + 1, :] for c in range(2)]
     layer_input = jnp.concatenate(
         [
@@ -317,18 +365,26 @@
     angle = 2.0 * np.pi * (np.outer(u, x) % grid) / grid
     table = np.where(np.arange(grid)[None] <= half, np.cos(angle), np.sin(angle)).astype(np.float32)
     back = (table.T / float(grid) ** 3).astype(np.float32)
-    return table, back
+
+    def halves(value):
+        high = value.astype(bf16)
+        low = (value - high.astype(np.float32)).astype(bf16)
+        return np.concatenate([high, high, low], axis=1)
+
+    return halves(table), halves(back)
 
 
 def reciprocal_kernel(
     grid, slabs, per_slab, second, depth,
     place_ref, exports_ref, payload_ref, green_ref, forward_ref, back_ref,
     out_ref,
-    planes, turns_high, turns_low, spread_high, spread_low, brick, carry,
+    planes_real, planes_imag, turns_high, turns_low, brick, carry,
     shift_cos, shift_sin, stage_cos, stage_sin, chosen, potential,
 ):
+    planes = (planes_real, planes_imag)
     domains = slabs * per_slab
     half = grid // 2
+    pitch = grid + 8
     thick = grid // slabs
     starts = thick - BX + 1
     rows = 2 * second
@@ -347,8 +403,6 @@
     shift_cos[...] = cosine
     shift_sin[...] = sine
     upper = rows_iota((rows, LANES)) >= second
-    spread_high[...] = jnp.zeros(spread_high.shape, bf16)
-    spread_low[...] = jnp.zeros(spread_low.shape, bf16)
     carry[...] = jnp.zeros(carry.shape, f32)
     left_half = lanes_iota((1, LANES)) < LANES // 2
 
@@ -371,48 +425,49 @@
             found.append(jnp.where(left_half, one, two))
         return jnp.concatenate(found, axis=1) if len(found) > 1 else found[0]
 
-    def fill_spread(slab):
-        both = []
+    def spread_of(slab):
+        both, pieces = [], []
         for t in range(chunks):
             parts = atom_rows(slab, t)
             along = windows(parts)
-            along_z = along[2]
-            masked = jnp.concatenate(
-                [jnp.where(left_half, along_z, 0.0), jnp.where(left_half, 0.0, along_z)], axis=0
-            )
-            high, low = split(masked)
-            spread_high[t * 16 : (t + 1) * 16, t * LANES : (t + 1) * LANES] = high
-            spread_low[t * 16 : (t + 1) * 16, t * LANES : (t + 1) * LANES] = low
+            pieces.append(jnp.where(left_half, along[2], 0.0))
+            pieces.append(jnp.where(left_half, 0.0, along[2]))
             both.append((parts, along))
-        return both
+        return both, split(jnp.concatenate(pieces, axis=0))
+
+    piece_of = lanes_iota((1, cells)) // (2 * BZ)
 
     def slab_masks(slab):
         start = anchor(slab, 0) - (slab * thick).astype(f32)
         return [(start == float(s)).astype(f32) for s in range(starts)]
 
-    def deposit(slab):
-        both = fill_spread(slab)
+    def deposit(slab, side):
+        both, spread = spread_of(slab)
         lefts = []
         for parts, (along_x, along_y, _) in both:
-            lefts.append(
-                jnp.concatenate(
-                    [(parts[c] * along_x[i]) * along_y for c in range(2) for i in range(BX)], axis=0
-                )
-            )
-        brick[...] = product(
-            split(jnp.concatenate(lefts, axis=1)), (spread_high[...], spread_low[...]), NT
-        )
+            for c in range(2):
+                for i in range(BX):
+                    lefts.append((parts[c] * along_x[i]) * along_y)
+        operand = split(jnp.concatenate(lefts, axis=0))
+        yield
+        found = product(operand, spread, NT)
+        yield
+        height = 2 * BX * BY
+        total = found[:height]
+        for t in range(1, chunks):
+            total = jnp.where(piece_of == t, found[t * height : (t + 1) * height], total)
+        brick[side] = total
         low_cell = anchor(slab, 2) + (lanes_iota((1, cells)) % BZ).astype(f32)
         ramp = rows_iota((8, cells)).astype(f32) + first_w
         cosine, sine = wave(ramp * low_cell, period)
         turn_cos, turn_sin = wave(8.0 * low_cell, period)
         for g in range(wide // 8):
             at = slice(g * 8, (g + 1) * 8)
-            stage_cos[at, :] = cosine
-            stage_sin[at, :] = sine
+            stage_cos[side, at, :] = cosine
+            stage_sin[side, at, :] = sine
             cosine, sine = cosine * turn_cos - sine * turn_sin, cosine * turn_sin + sine * turn_cos
-        cos_high, cos_low = split(stage_cos[...])
-        sin_high, sin_low = split(stage_sin[...])
+        cos_high, cos_low = split(stage_cos[side])
+        sin_high, sin_low = split(stage_sin[side])
         for ref, c_part, s_part in ((turns_high, cos_high, sin_high), (turns_low, cos_low, sin_low)):
             ref[slab, :wide, :cells] = c_part
             ref[slab, :wide, cells:] = s_part
@@ -426,8 +481,8 @@
         imag = [jnp.zeros((rows, cells), f32)] * BX
         for j in range(BY):
             for i in range(BX):
-                low = brick[i * BY + j : i * BY + j + 1, :]
-                high = brick[(BX + i) * BY + j : (BX + i) * BY + j + 1, :]
+                low = brick[side, i * BY + j : i * BY + j + 1, :]
+                high = brick[side, (BX + i) * BY + j : (BX + i) * BY + j + 1, :]
                 weight = jnp.where(top, high, low)
                 real[i] = real[i] + weight * cosine
                 imag[i] = imag[i] - weight * sine
@@ -448,33 +503,38 @@
                         total = piece if total is None else total + piece
                 parts.append(total)
             placed.append(jnp.concatenate(parts, axis=1))
-        return product(
-            split(jnp.concatenate(placed, axis=0)), (turns_high[slab], turns_low[slab]), NT
-        )
+        operand = split(jnp.concatenate(placed, axis=0))
+        yield
+        return product(operand, (turns_high[slab], turns_low[slab]), NT)
 
     def put(x, value):
-        planes[:, pl.ds(x, 1), :] = value[:, None, :]
+        for part, ref in enumerate(planes):
+            ref[pl.ds(x, rows, stride=pitch), :] = value[:, part * wide : (part + 1) * wide]
 
     def get(x):
-        return planes[:, pl.ds(x, 1), :][:, 0, :]
+        return jnp.concatenate([ref[pl.ds(x, rows, stride=pitch), :] for ref in planes], axis=1)
 
     def swapped(value):
         return jnp.concatenate([value[:, wide:], -value[:, :wide]], axis=1)
 
-    @pl.loop(0, slabs // 2)
-    def _(m):
-        near = deposit(m)
-        far = deposit(slabs - 1 - m)
-        for r in range(thick):
-            x = m * thick + r
-            one = near[r * rows : (r + 1) * rows]
-            if r == 0:
-                two = carry[...]
-            else:
-                two = far[(thick - r) * rows : (thick - r + 1) * rows]
-            put(x, one + two)
-            put(half + x, swapped(one - two))
-        carry[...] = far[:rows]
+    pairs = 2 if slabs % 4 == 0 else 1
+
+    @pl.loop(0, slabs // 2 // pairs)
+    def _(step):
+        first = [step * pairs + n for n in range(pairs)]
+        both = [slab for m in first for slab in (m, slabs - 1 - m)]
+        found = side_by_side([deposit(slab, side) for side, slab in enumerate(both)])
+        last = carry[...]
+        for n, m in enumerate(first):
+            near, far = found[2 * n], found[2 * n + 1]
+            for r in range(thick):
+                x = m * thick + r
+                one = near[r * rows : (r + 1) * rows]
+                two = last if r == 0 else far[(thick - r) * rows : (thick - r + 1) * rows]
+                put(x, one + two)
+                put(half + x, swapped(one - two))
+            last = far[:rows]
+        carry[...] = last
 
     put(half, carry[...])
 
@@ -484,38 +544,54 @@
             return kernel
         return jnp.concatenate([kernel, jnp.zeros((kernel.shape[0], gap), f32)], axis=1)
 
-    table = split(forward_ref[...])
-    table_back = split(back_ref[...])
-
-    @pl.loop(0, second)
-    def _(v):
-        inside = jnp.concatenate([planes[v], planes[second + v]], axis=1)
-        spectrum = product(table, split(inside))
+    def transformed(table_ref, value):
+        high, low = split(value)
+        return lax.dot_general(
+            table_ref[...], jnp.concatenate([high, low, high], axis=0), NN, preferred_element_type=f32
+        )
+
+    together = 2 if second % 2 == 0 else 1
+
+    @pl.loop(0, second // together)
+    def _(step):
+        frequencies = [step * together + n for n in range(together)]
+        places = [
+            pl.ds(pl.multiple_of((c * second + v) * pitch, 8), grid)
+            for v in frequencies
+            for c in range(2)
+        ]
+        inside = jnp.concatenate([ref[place, :] for place in places for ref in planes], axis=1)
+        spectrum = transformed(forward_ref, inside)
         outside = []
-        for c in range(2):
-            zero, one = padded(green_ref[v, c, 0]), padded(green_ref[v, c, 1])
-            for part in range(2):
-                outside.append(
-                    zero * spectrum[:, part * wide : (part + 1) * wide]
-                    + one * spectrum[:, (2 + part) * wide : (3 + part) * wide]
-                )
-        result = product(table_back, split(jnp.concatenate(outside, axis=1)))
-        planes[v] = result[:, : 2 * wide]
-        planes[second + v] = result[:, 2 * wide :]
-
-    def evaluate(slab, inputs):
+        for n, v in enumerate(frequencies):
+            for c in range(2):
+                zero, one = padded(green_ref[v, c, 0]), padded(green_ref[v, c, 1])
+                for part in range(2):
+                    at = (4 * n + part) * wide
+                    outside.append(
+                        zero * spectrum[:, at : at + wide]
+                        + one * spectrum[:, at + 2 * wide : at + 3 * wide]
+                    )
+        result = transformed(back_ref, jnp.concatenate(outside, axis=1))
+        for n, place in enumerate(places):
+            for part, ref in enumerate(planes):
+                at = (2 * n + part) * wide
+                ref[place, :] = result[:, at : at + wide]
+
+    def evaluate(slab, inputs, side):
         masks = slab_masks(slab)
-        both = fill_spread(slab)
-        found = product(
-            split(jnp.concatenate(inputs, axis=0)), (turns_high[slab], turns_low[slab])
-        )
+        both, spread = spread_of(slab)
+        operand = split(jnp.concatenate(inputs, axis=0))
+        yield
+        found = product(operand, (turns_high[slab], turns_low[slab]))
+        yield
         twice = [jnp.concatenate([mask, mask], axis=1) for mask in masks]
         for i in range(BX):
             total = None
             for s in range(starts):
                 piece = found[(s + i) * rows : (s + i + 1) * rows] * twice[s]
                 total = piece if total is None else total + piece
-            chosen[i * rows : (i + 1) * rows, :] = total
+            chosen[side, i * rows : (i + 1) * rows, :] = total
         cell = anchor(slab, 1) + rows_iota((BY, cells)).astype(f32)
         cosine, sine = wave(cell * first_v, period)
         turn_cos, turn_sin = wave(cell, period)
@@ -526,23 +602,25 @@
                     at = i * rows + c * second + v
                     sums[c * BX + i] = (
                         sums[c * BX + i]
-                        + chosen[at : at + 1, :cells] * cosine
-                        - chosen[at : at + 1, cells:] * sine
+                        + chosen[side, at : at + 1, :cells] * cosine
+                        - chosen[side, at : at + 1, cells:] * sine
                     )
             if v + 1 < second:
                 cosine, sine = cosine * turn_cos - sine * turn_sin, cosine * turn_sin + sine * turn_cos
-        at_atoms = product(
-            split(jnp.concatenate(sums, axis=0)), (spread_high[...], spread_low[...])
-        )
+        summed = jnp.concatenate(sums, axis=0)
+        masked = [jnp.where(piece_of == t, summed, 0.0) for t in range(chunks)]
+        operand = split(jnp.concatenate(masked, axis=0))
+        yield
+        at_atoms = product(operand, spread)
+        yield
         for t in range(chunks):
-            lane = slice(t * LANES, (t + 1) * LANES)
             _, (along_x, along_y, _) = both[t]
             pair = []
             for c in range(2):
                 total = None
                 for i in range(BX):
-                    at = (c * BX + i) * BY
-                    piece = at_atoms[at : at + BY, lane] * along_x[i]
+                    at = (t * 2 * BX + c * BX + i) * BY
+                    piece = at_atoms[at : at + BY] * along_x[i]
                     total = piece if total is None else total + piece
                 pair.append(jnp.sum(total * along_y, axis=0, keepdims=True))
             one = jnp.where(left_half, pair[0], pltpu.roll(pair[1], LANES // 2, 1))
@@ -556,17 +634,21 @@
         turned = jnp.concatenate([-odd[:, wide:], odd[:, :wide]], axis=1)
         return even + turned, even - turned
 
-    @pl.loop(0, slabs // 2)
-    def _(m):
-        near, far = [], [None] * thick
-        for r in range(thick):
-            ahead, behind = straight(m * thick + r)
-            near.append(ahead)
-            if r > 0:
-                far[thick - r] = behind
-        far[0] = straight(m * thick + thick)[1]
-        evaluate(m, near)
-        evaluate(slabs - 1 - m, far)
+    @pl.loop(0, slabs // 2 // pairs)
+    def _(step):
+        works = []
+        for n in range(pairs):
+            m = step * pairs + n
+            near, far = [], [None] * thick
+            for r in range(thick):
+                ahead, behind = straight(m * thick + r)
+                near.append(ahead)
+                if r > 0:
+                    far[thick - r] = behind
+            far[0] = straight(m * thick + thick)[1]
+            works.append(evaluate(m, near, 2 * n))
+            works.append(evaluate(slabs - 1 - m, far, 2 * n + 1))
+        side_by_side(works)
 
     @pl.loop(0, domains)
     def _(domain):
@@ -584,25 +666,23 @@
 def build_reciprocal(grid, slabs, per_slab, second, depth):
     domains = slabs * per_slab
     cells = per_slab * NB * BZ
-    slab_atoms = per_slab * NB * BA
     return pl.pallas_call(
         functools.partial(reciprocal_kernel, grid, slabs, per_slab, second, depth),
         in_specs=[SMEM, SMEM] + [VMEM] * 4,
         out_specs=VMEM,
         out_shape=jax.ShapeDtypeStruct((domains, 16, LANES), f32),
         scratch_shapes=[
-            pltpu.VMEM((2 * second, grid, 2 * depth), f32),
+            pltpu.VMEM((2 * second * (grid + 8), depth), f32),
+            pltpu.VMEM((2 * second * (grid + 8), depth), f32),
             pltpu.VMEM((slabs, 2 * depth, 2 * cells), bf16),
             pltpu.VMEM((slabs, 2 * depth, 2 * cells), bf16),
-            pltpu.VMEM((cells, slab_atoms), bf16),
-            pltpu.VMEM((cells, slab_atoms), bf16),
-            pltpu.VMEM((2 * BX * BY, cells), f32),
+            pltpu.VMEM((4, 2 * BX * BY, cells), f32),
             pltpu.VMEM((2 * second, 2 * depth), f32),
             pltpu.VMEM((2 * second, LANES), f32),
             pltpu.VMEM((2 * second, LANES), f32),
-            pltpu.VMEM((depth, cells), f32),
-            pltpu.VMEM((depth, cells), f32),
-            pltpu.VMEM((BX * 2 * second, 2 * cells), f32),
+            pltpu.VMEM((4, depth, cells), f32),
+            pltpu.VMEM((4, depth, cells), f32),
+            pltpu.VMEM((4, BX * 2 * second, 2 * cells), f32),
             pltpu.VMEM((domains * NB, LANES), f32),
         ],
         compiler_params=params(),
@@ -656,28 +736,35 @@
         compiler_params=params(),
     )(features, positions, charge_weight, brick_anchor, exports, export_counts)
 
-    up, down, green_kernel = lax.optimization_barrier((up, down, green_kernel))
-    green = jnp.transpose(green_kernel, (4, 1, 2, 3, 0))
+    everyone = lax.all_to_all(payload, axes, 0, 0, tiled=True)
+    up, down, green_kernel, features = lax.optimization_barrier((up, down, green_kernel, features))
     up = around(up, 1)
     down = around(down, -1)
-    payload, green, up, down = lax.optimization_barrier((payload, green, up, down))
-    everyone = lax.all_to_all(payload, axes, 0, 0, tiled=True)
+    green = jnp.transpose(green_kernel, (4, 1, 2, 3, 0))
+    own = pl.pallas_call(
+        first_own_kernel,
+        in_specs=[VMEM] * 4,
+        out_specs=VMEM,
+        out_shape=shape(atoms, width),
+        scratch_shapes=[pltpu.VMEM((atoms, width), f32)],
+        compiler_params=params(),
+    )(features, positions, value_one, radial_one)
+    own, green, up, down = lax.optimization_barrier((own, green, up, down))
 
     hidden, values_two, up_two, down_two, ghost_places = pl.pallas_call(
         first_layer_kernel,
-        in_specs=[VMEM] * 8 + [SMEM],
+        in_specs=[VMEM] * 9 + [SMEM],
         out_specs=[VMEM] * 5,
         out_shape=[
             shape(atoms, width), shape(atoms, width), shape(base, width), shape(base, width),
             shape(8, width),
         ],
         scratch_shapes=[
-            pltpu.VMEM((atoms, width), f32),
             pltpu.VMEM((2 * base, width), f32),
             pltpu.VMEM((atoms, width), f32),
         ],
         compiler_params=params(),
-    )(features, up, down, positions, value_one, output_one, radial_one, value_two, exports)
+    )(features, own, up, down, positions, value_one, output_one, radial_one, value_two, exports)
 
     everyone, hidden = lax.optimization_barrier((everyone, hidden))
     up_two = around(up_two, 1)

time: 120 us -> 103 us (0.86)
  Pallas kernels: 80.4 us -> 64.5 us
  waiting for transfers between devices: 7.24 us -> 5.19 us
    pallas_call x1, Pallas kernels: 43 us -> 24 us  [per_device(): build_reciprocal(grid, slabs, per_slab, second, depth)]
    pallas_call x1 -> x2, Pallas kernels: 15.4 us -> 18.6 us  [the longest x1 12.5 us: per_device(): pl.pallas_call(first_layer_kernel, in_specs=[VMEM] * 9 + [SMEM], out_spec...]
    ppermute x4, waiting for transfers between devices: 7.24 us -> 5.18 us  [around(): lax.ppermute(rows, axes, [(i, (i + by) % domains) for i in range(domains)])]
    all_to_all x1, starting transfers between devices: 5.82 us -> 7.3 us  [per_device(): everyone = lax.all_to_all(payload, axes, 0, 0, tiled=True)]
  transfers between devices with their start and end apart: 6 -> 6, of which waited for: 2 -> 1; matrix products, arithmetic and copies ran while one was open for 8% -> 9% of each run, Pallas kernels for 59% -> 53%
where the time goes in v2:
time: 103 us; the launch traced here: 102 us
  Pallas kernels  64.5 us (63%)
  starting transfers between devices  20.6 us (20%)
  local copies, waits for them, and re-layouts  10.8 us (10%)
  waiting for transfers between devices  5.19 us (5%)
  other arithmetic  1.3 us (1%)
    pallas_call x1, Pallas kernels, per_device(): build_reciprocal(grid, slabs, per_slab, second, depth)  24 us
    pallas_call x1, Pallas kernels, per_device(): pl.pallas_call(first_layer_kernel, in_specs=[VMEM] * 9 + [SMEM], out_spec...  12.5 us
    pallas_call x1, Pallas kernels, per_device(): pl.pallas_call(second_layer_kernel, in_specs=[VMEM] * 8, out_specs=[VMEM]...  11.4 us
    ppermute x4, starting transfers between devices, around(): lax.ppermute(rows, axes, [(i, (i + by) % domains) for i in range(domains)])  10.7 us
    optimization_barrier x1, local copies, waits for them, and re-layouts, per_device(): lax.optimization_barrier((up, down, green_kernel, features))  7.73 us
    all_to_all x1, starting transfers between devices, per_device(): everyone = lax.all_to_all(payload, axes, 0, 0, tiled=True)  7.3 us
    pallas_call x1, Pallas kernels, per_device(): pl.pallas_call(tail_kernel, in_specs=[VMEM] * 9, out_specs=VMEM, out_shap...  7.21 us
    pallas_call x1, Pallas kernels, per_device(): pl.pallas_call(first_own_kernel, in_specs=[VMEM] * 4, out_specs=VMEM, out...  6.16 us
  transfers between devices with their start and end apart: 6, of which 1 were waited for; matrix products, arithmetic and copies ran while one was open for 9% of the time, Pallas kernels for 53%

profile of v2, /device:TPU:0, one launch (start us, length us, event | category | flops | bytes accessed | tf_op | source)
XLA Modules:
  0.0 102.5 jit_solution(13398319021454366194)
XLA Ops:
  0.0 1.5 %copy.17.charge_ref = f32[512,2]{1,0:T(8,128)} copy(f32[512,2]{0,1:T(2,128)} %param.24) | data formatting | bytes 8192 | tf_op args[8]
  1.5 3.2 %shard_map.154 = (f32[200,512]{1,0:T(8,128)}, f32[200,512]{1,0:T(8,128)}, f32[32,24,128]{2,1,0:T(8,128)}) custom-call(f32[512,512]{1,0:T(8,128)} %features_ref.3, f32[3,512]{1,0:T(4,128)} %places_ref.9, f32[512,2]{1,0:T(8,128)} %copy.17.charge_ref, s32[3,8]{1,0:T(4,128)} %anchor_ref.1, s32[1,2,3]{2,1,0:T(2,128)} %exports_ref.3, s32[1,2]{1,0:T(1,128)} %counts_ref.1), custom_call_target="tpu_custom_call" | custom-call | tf_op jit(solution)/shard_map/pallas_call | solution.py:728
  4.8 7.3 %all-to-all-start = ((f32[32,24,128]{2,1,0:T(8,128)}), f32[32,24,128]{2,1,0:T(8,128)S(1)}, u32[]{:S(2)}, u32[]{:S(2)}) async-start(f32[32,24,128]{2,1,0:T(8,128)} %get-tuple-element.28), calls=%async_computation | async-start | bytes 786432 | tf_op jit(solution)/shard_map/all_to_all | solution.py:739
  12.1 1.8 %collective-permute-start = (f32[200,512]{1,0:T(8,128)}, f32[200,512]{1,0:T(8,128)S(1)}, u32[]{:S(2)}, u32[]{:S(2)}) collective-permute-start(f32[200,512]{1,0:T(8,128)} %get-tuple-element.33), channel_id=1, source_target_pairs={{0,1},{1,2},{2,3},{3,4},{4,5},{5,6},{6,7},{7,8},{8,9},{9,10},{10,1... | collective-permute-start | bytes 1228808 | tf_op jit(solution)/shard_map/ppermute | solution.py:726
  13.9 3.6 %collective-permute-start.1 = (f32[200,512]{1,0:T(8,128)}, f32[200,512]{1,0:T(8,128)S(1)}, u32[]{:S(2)}, u32[]{:S(2)}) collective-permute-start(f32[200,512]{1,0:T(8,128)} %get-tuple-element.34), channel_id=1, source_target_pairs={{0,31},{1,0},{2,1},{3,2},{4,3},{5,4},{6,5},{7,6},{8,7},{9,8},{10,9... | collective-permute-start | bytes 1228808 | tf_op jit(solution)/shard_map/ppermute | solution.py:726
  17.5 7.7 %copy.18 = f32[96,2,2,192,12]{0,3,2,1,4:T(8,128)} copy(f32[96,2,2,192,12]{3,2,4,1,0:T(2,128)} %param.26) | data formatting | bytes 7077888 | tf_op jit(solution)/shard_map/optimization_barrier | solution.py:740
  25.2 6.2 %shard_map.155.own_ref = f32[512,512]{1,0:T(8,128)} custom-call(f32[512,512]{1,0:T(8,128)} %features_ref.3, f32[3,512]{1,0:T(4,128)} %places_ref.9, f32[512,512]{1,0:T(8,128)} %value_one_ref.3, f32[8,512]{1,0:T(8,128)} %weight_ref.5), custom_call_target="tpu_custom_call" | custom-call | tf_op jit(solution)/shard_map/pallas_call | solution.py:744
  31.4 0.0 collective-permute-done.up_ref
  31.4 0.0 copy-start.2
  31.4 5.2 %collective-permute-done.1.down_ref = f32[200,512]{1,0:T(8,128)S(1)} collective-permute-done((f32[200,512]{1,0:T(8,128)}, f32[200,512]{1,0:T(8,128)S(1)}, u32[]{:S(2)}, u32[]{:S(2)}) %collective-permute-start.1) | collective-permute-done | bytes 409632 | tf_op jit(solution)/shard_map/ppermute | solution.py:726
  36.6 0.0 copy-start.3
  36.6 0.0 copy-done.2
  36.6 0.7 copy-done.3
  37.3 12.5 %shard_map.156 = (f32[512,512]{1,0:T(8,128)}, f32[512,512]{1,0:T(8,128)}, f32[192,512]{1,0:T(8,128)}, f32[192,512]{1,0:T(8,128)}, f32[8,512]{1,0:T(8,128)}) custom-call(f32[512,512]{1,0:T(8,128)} %features_ref.3, f32[512,512]{1,0:T(8,128)} %shard_map.155.own_ref, f32[200,512]{1,0:T(8,128)} %copy-done.2, f32[200,512]{1,0:T(8,128)} %copy-done.3, ...), custom_call_target="tpu_custom_call" | custom-call | tf_op jit(solution)/shard_map/pallas_call | solution.py:754
  49.8 0.7 collective-permute-start.2
  50.5 4.6 %collective-permute-start.3 = (f32[192,512]{1,0:T(8,128)}, f32[192,512]{1,0:T(8,128)S(1)}, u32[]{:S(2)}, u32[]{:S(2)}) collective-permute-start(f32[192,512]{1,0:T(8,128)} %get-tuple-element.42), channel_id=1, source_target_pairs={{0,31},{1,0},{2,1},{3,2},{4,3},{5,4},{6,5},{7,6},{8,7},{9,8},{10,9... | collective-permute-start | bytes 1179656 | tf_op jit(solution)/shard_map/ppermute | solution.py:726
  55.1 0.6 pad_add_fusion.place_ref
  55.7 0.0 all-to-all-done.payload_ref
  55.7 0.0 copy-start
  55.7 0.7 slice_convert_fusion
  56.4 0.1 copy-done
  56.5 24.0 %shard_map.157 = f32[32,16,128]{2,1,0:T(8,128)} custom-call(s32[3]{0:T(128)} %pad_add_fusion.place_ref, s32[32,8]{1,0:T(8,128)} %bitcast.5, f32[32,24,128]{2,1,0:T(8,128)} %copy-done, f32[12,2,2,192,96]{4,3,2,1,0:T(8,128)} %bitcast.4, bf16[192,576]{1,0:T(8,128)(2,1)} %constant.14.clone.forward_ref, bf16[192,576]{1,0:T(8,128)(2,1)} %constant.15.clone.back_ref), custom_call_target="tpu_custom_call" | custom-call | tf_op jit(solution)/shard_map/pallas_call | solution.py:778
  80.5 0.0 collective-permute-done.2.up_two_ref
  80.5 0.0 copy-start.4
  80.5 0.0 collective-permute-done.3.down_two_ref
  80.5 0.0 copy-start.5
  80.5 2.6 %all-to-all-start.1 = ((f32[32,16,128]{2,1,0:T(8,128)}), f32[32,16,128]{2,1,0:T(8,128)S(1)}, u32[]{:S(2)}, u32[]{:S(2)}) async-start(f32[32,16,128]{2,1,0:T(8,128)} %shard_map.157), calls=%async_computation.1 | async-start | bytes 524288 | tf_op jit(solution)/shard_map/all_to_all | solution.py:783
  83.2 0.0 copy-done.4
  83.2 0.0 copy-done.5
  83.2 11.4 %shard_map.158 = (f32[512,512]{1,0:T(8,128)}, f32[8,512]{1,0:T(8,128)}) custom-call(f32[512,512]{1,0:T(8,128)} %get-tuple-element.44.values_ref, f32[192,512]{1,0:T(8,128)} %copy-done.4, f32[192,512]{1,0:T(8,128)} %copy-done.5, f32[8,512]{1,0:T(8,128)} %get-tuple-element.47.ghost_places_ref, f32[3,512]{1,0:T(4,128)} %places_ref.9, f32[8,512]{1,0:T(8,128)} %weight_ref.7, ...), custom_call_target="tpu_custom_call" | custom-call | tf_op jit(solution)/shard_map/pallas_call | solution.py:785
  94.6 0.0 all-to-all-done.1.received_ref
  94.6 0.0 copy-start.1
  94.6 0.7 copy-done.1
  95.3 7.2 %shard_map.159 = f32[512,512]{1,0:T(8,128)} custom-call(f32[32,16,128]{2,1,0:T(8,128)} %copy-done.1, f32[512,512]{1,0:T(8,128)} %get-tuple-element.48.messages_ref, f32[512,512]{1,0:T(8,128)} %get-tuple-element.49.hidden_ref, f32[8,512]{1,0:T(8,128)} %get-tuple-element.47.ghost_places_ref, f32[3,512]{1,0:T(4,128)} %places_ref.9, f32[8,512]{1,0:T(8,128)} %weight_ref.7, ...), custom_call_target="tpu_custom_call" | custom-call | tf_op jit(solution)/shard_map/pallas_call | solution.py:794
Async XLA Ops:
  4.8 51.0 %all-to-all-start = ((f32[32,24,128]{2,1,0:T(8,128)}), f32[32,24,128]{2,1,0:T(8,128)S(1)}, u32[]{:S(2)}, u32[]{:S(2)}) async-start(f32[32,24,128]{2,1,0:T(8,128)} %get-tuple-element.28), calls=%async_computation | async-start | bytes 786432 | tf_op jit(solution)/shard_map/all_to_all | solution.py:739
  12.1 19.3 %collective-permute-start = (f32[200,512]{1,0:T(8,128)}, f32[200,512]{1,0:T(8,128)S(1)}, u32[]{:S(2)}, u32[]{:S(2)}) collective-permute-start(f32[200,512]{1,0:T(8,128)} %get-tuple-element.33), channel_id=1, source_target_pairs={{0,1},{1,2},{2,3},{3,4},{4,5},{5,6},{6,7},{7,8},{8,9},{9,10},{10,1... | collective-permute-start | bytes 1228808 | tf_op jit(solution)/shard_map/ppermute | solution.py:726
  13.9 22.7 %collective-permute-start.1 = (f32[200,512]{1,0:T(8,128)}, f32[200,512]{1,0:T(8,128)S(1)}, u32[]{:S(2)}, u32[]{:S(2)}) collective-permute-start(f32[200,512]{1,0:T(8,128)} %get-tuple-element.34), channel_id=1, source_target_pairs={{0,31},{1,0},{2,1},{3,2},{4,3},{5,4},{6,5},{7,6},{8,7},{9,8},{10,9... | collective-permute-start | bytes 1228808 | tf_op jit(solution)/shard_map/ppermute | solution.py:726
  31.4 5.2 %copy-start.2 = (f32[200,512]{1,0:T(8,128)}, f32[200,512]{1,0:T(8,128)S(1)}, u32[]{:S(2)}) copy-start(f32[200,512]{1,0:T(8,128)S(1)} %collective-permute-done.up_ref) | copy-start | bytes 1228804
  36.6 0.8 copy-start.3
  49.8 30.8 %collective-permute-start.2 = (f32[192,512]{1,0:T(8,128)}, f32[192,512]{1,0:T(8,128)S(1)}, u32[]{:S(2)}, u32[]{:S(2)}) collective-permute-start(f32[192,512]{1,0:T(8,128)} %get-tuple-element.41), channel_id=1, source_target_pairs={{0,1},{1,2},{2,3},{3,4},{4,5},{5,6},{6,7},{7,8},{8,9},{9,10},{10,1... | collective-permute-start | bytes 1179656 | tf_op jit(solution)/shard_map/ppermute | solution.py:726
  50.5 30.0 %collective-permute-start.3 = (f32[192,512]{1,0:T(8,128)}, f32[192,512]{1,0:T(8,128)S(1)}, u32[]{:S(2)}, u32[]{:S(2)}) collective-permute-start(f32[192,512]{1,0:T(8,128)} %get-tuple-element.42), channel_id=1, source_target_pairs={{0,31},{1,0},{2,1},{3,2},{4,3},{5,4},{6,5},{7,6},{8,7},{9,8},{10,9... | collective-permute-start | bytes 1179656 | tf_op jit(solution)/shard_map/ppermute | solution.py:726
  55.7 0.8 copy-start
  80.5 2.6 %copy-start.4 = (f32[192,512]{1,0:T(8,128)}, f32[192,512]{1,0:T(8,128)S(1)}, u32[]{:S(2)}) copy-start(f32[192,512]{1,0:T(8,128)S(1)} %collective-permute-done.2.up_two_ref) | copy-start | bytes 1179652
  80.5 2.6 %copy-start.5 = (f32[192,512]{1,0:T(8,128)}, f32[192,512]{1,0:T(8,128)S(1)}, u32[]{:S(2)}) copy-start(f32[192,512]{1,0:T(8,128)S(1)} %collective-permute-done.3.down_two_ref) | copy-start | bytes 1179652
  80.5 14.0 %all-to-all-start.1 = ((f32[32,16,128]{2,1,0:T(8,128)}), f32[32,16,128]{2,1,0:T(8,128)S(1)}, u32[]{:S(2)}, u32[]{:S(2)}) async-start(f32[32,16,128]{2,1,0:T(8,128)} %shard_map.157), calls=%async_computation.1 | async-start | bytes 524288 | tf_op jit(solution)/shard_map/all_to_all | solution.py:783
  94.6 0.7 copy-start.1

commit v3 on v2

--- a/solution.py
+++ b/solution.py
@@ -116,9 +116,8 @@
     for out_ref, side in ((up_ref, 0), (down_ref, 1)):
         pack_rows(out_ref, features_ref, exports_ref, side)
         pack_places(out_ref, places_ref, exports_ref, counts_ref, side)
-    width = charge_ref.shape[0]
-    charge_rows = jnp.transpose(
-        jnp.concatenate([charge_ref[...], jnp.zeros((width, 6), f32)], axis=1)
+    charge_rows = jnp.concatenate(
+        [charge_ref[...], jnp.zeros((6, charge_ref.shape[1]), f32)], axis=0
     )
     charges = product(split(charge_rows), split(features_ref[...]), NT)
     chunks = features_ref.shape[0] // LANES
@@ -153,7 +152,7 @@
     near = jnp.exp(-2.0 * softened)
     if live is not None:
         near = near * live
-    return near, jnp.exp(STEP * jnp.sqrt(softened))
+    return near, jnp.exp(STEP * (softened * lax.rsqrt(softened)))
 
 
 def squared_distance(columns, rows):
@@ -376,11 +375,13 @@
 
 def reciprocal_kernel(
     grid, slabs, per_slab, second, depth,
-    place_ref, exports_ref, payload_ref, green_ref, forward_ref, back_ref,
+    place_ref, exports_ref, payload_ref, green_hbm, forward_ref, back_ref,
     out_ref,
-    planes_real, planes_imag, turns_high, turns_low, brick, carry,
+    green_ref, green_arrived, planes_real, planes_imag, turns_high, turns_low, brick, carry,
     shift_cos, shift_sin, stage_cos, stage_sin, chosen, potential,
 ):
+    green_copy = pltpu.make_async_copy(green_hbm, green_ref, green_arrived)
+    green_copy.start()
     planes = (planes_real, planes_imag)
     domains = slabs * per_slab
     half = grid // 2
@@ -517,7 +518,7 @@
     def swapped(value):
         return jnp.concatenate([value[:, wide:], -value[:, :wide]], axis=1)
 
-    pairs = 2 if slabs % 4 == 0 else 1
+    pairs = pairs_of(slabs, per_slab)
 
     @pl.loop(0, slabs // 2 // pairs)
     def _(step):
@@ -537,6 +538,7 @@
         carry[...] = last
 
     put(half, carry[...])
+    green_copy.wait()
 
     def padded(kernel):
         gap = wide - kernel.shape[1]
@@ -663,26 +665,35 @@
             out_ref[domain, NB + NH + s : NB + NH + s + 1, :] = potential[pl.ds(at, 1), :]
 
 
-def build_reciprocal(grid, slabs, per_slab, second, depth):
+def pairs_of(slabs, per_slab):
+    if per_slab <= 2 and slabs % 8 == 0:
+        return 4
+    return 2 if slabs % 4 == 0 else 1
+
+
+def build_reciprocal(grid, slabs, per_slab, second, depth, depth_rows):
     domains = slabs * per_slab
     cells = per_slab * NB * BZ
+    sides = 2 * pairs_of(slabs, per_slab)
     return pl.pallas_call(
         functools.partial(reciprocal_kernel, grid, slabs, per_slab, second, depth),
-        in_specs=[SMEM, SMEM] + [VMEM] * 4,
+        in_specs=[SMEM, SMEM, VMEM, pl.BlockSpec(memory_space=pl.ANY), VMEM, VMEM],
         out_specs=VMEM,
         out_shape=jax.ShapeDtypeStruct((domains, 16, LANES), f32),
         scratch_shapes=[
+            pltpu.VMEM((second, 2, 2, grid, depth_rows), f32),
+            pltpu.SemaphoreType.DMA,
             pltpu.VMEM((2 * second * (grid + 8), depth), f32),
             pltpu.VMEM((2 * second * (grid + 8), depth), f32),
             pltpu.VMEM((slabs, 2 * depth, 2 * cells), bf16),
             pltpu.VMEM((slabs, 2 * depth, 2 * cells), bf16),
-            pltpu.VMEM((4, 2 * BX * BY, cells), f32),
+            pltpu.VMEM((sides, 2 * BX * BY, cells), f32),
             pltpu.VMEM((2 * second, 2 * depth), f32),
             pltpu.VMEM((2 * second, LANES), f32),
             pltpu.VMEM((2 * second, LANES), f32),
-            pltpu.VMEM((4, depth, cells), f32),
-            pltpu.VMEM((4, depth, cells), f32),
-            pltpu.VMEM((4, BX * 2 * second, 2 * cells), f32),
+            pltpu.VMEM((sides, depth, cells), f32),
+            pltpu.VMEM((sides, depth, cells), f32),
+            pltpu.VMEM((sides, BX * 2 * second, 2 * cells), f32),
             pltpu.VMEM((domains * NB, LANES), f32),
         ],
         compiler_params=params(),
@@ -734,13 +745,11 @@
         ],
         scratch_shapes=[pltpu.VMEM((payload_rows, LANES), f32)],
         compiler_params=params(),
-    )(features, positions, charge_weight, brick_anchor, exports, export_counts)
-
-    everyone = lax.all_to_all(payload, axes, 0, 0, tiled=True)
-    up, down, green_kernel, features = lax.optimization_barrier((up, down, green_kernel, features))
+    )(features, positions, charge_weight.T, brick_anchor, exports, export_counts)
+
+    up, down, features, green_kernel = lax.optimization_barrier((up, down, features, green_kernel))
     up = around(up, 1)
     down = around(down, -1)
-    green = jnp.transpose(green_kernel, (4, 1, 2, 3, 0))
     own = pl.pallas_call(
         first_own_kernel,
         in_specs=[VMEM] * 4,
@@ -749,7 +758,9 @@
         scratch_shapes=[pltpu.VMEM((atoms, width), f32)],
         compiler_params=params(),
     )(features, positions, value_one, radial_one)
-    own, green, up, down = lax.optimization_barrier((own, green, up, down))
+    green = jnp.transpose(green_kernel, (4, 1, 2, 3, 0))
+    payload, own, green, up, down = lax.optimization_barrier((payload, own, green, up, down))
+    everyone = lax.all_to_all(payload, axes, 0, 0, tiled=True)
 
     hidden, values_two, up_two, down_two, ghost_places = pl.pallas_call(
         first_layer_kernel,
@@ -775,7 +786,7 @@
     ).astype(jnp.int32)
     all_exports = everyone[:, 5 * chunks + 3, :8].astype(jnp.int32)
     table, table_back = transform_tables(grid)
-    outgoing = build_reciprocal(grid, slabs, per_slab, second, depth)(
+    outgoing = build_reciprocal(grid, slabs, per_slab, second, depth, depth_rows)(
         place, all_exports, everyone, green, table, table_back
     )
 

time: 103 us -> 93.8 us (0.911)
  waiting for transfers between devices: 5.19 us -> 1.1 us
  Pallas kernels: 64.5 us -> 61.7 us
  local copies, waits for them, and re-layouts: 10.8 us -> 8.54 us
    ppermute x4, waiting for transfers between devices: 5.18 us -> 1.1 us  [around(): lax.ppermute(rows, axes, [(i, (i + by) % domains) for i in range(domains)])]
    unnamed x13 -> x12, local copies, waits for them, and re-layouts: 3.09 us -> 0.81 us
    pallas_call x1, Pallas kernels: 24 us -> 21.8 us  [per_device(): build_reciprocal(grid, slabs, per_slab, second, depth, depth_rows)]
    all_to_all x1, starting transfers between devices: 7.3 us -> 5.82 us  [per_device(): everyone = lax.all_to_all(payload, axes, 0, 0, tiled=True)]
    ppermute x4, starting transfers between devices: 10.7 us -> 11.8 us  [around(): lax.ppermute(rows, axes, [(i, (i + by) % domains) for i in range(domains)])]
  transfers between devices with their start and end apart: 6 -> 6, of which waited for: 1 -> 1; matrix products, arithmetic and copies ran while one was open for 9% -> 10% of each run, Pallas kernels for 53% -> 55%
where the time goes in v3:
time: 93.8 us; the launch traced here: 93.2 us
  Pallas kernels  61.7 us (66%)
  starting transfers between devices  20.5 us (22%)
  local copies, waits for them, and re-layouts  8.54 us (9%)
  other arithmetic  1.3 us (1%)
  waiting for transfers between devices  1.1 us (1%)
    pallas_call x1, Pallas kernels, per_device(): build_reciprocal(grid, slabs, per_slab, second, depth, depth_rows)  21.8 us
    pallas_call x1, Pallas kernels, per_device(): pl.pallas_call(first_layer_kernel, in_specs=[VMEM] * 9 + [SMEM], out_spec...  12.3 us
    ppermute x4, starting transfers between devices, around(): lax.ppermute(rows, axes, [(i, (i + by) % domains) for i in range(domains)])  11.8 us
    pallas_call x1, Pallas kernels, per_device(): pl.pallas_call(second_layer_kernel, in_specs=[VMEM] * 8, out_specs=[VMEM]...  11.2 us
    optimization_barrier x1, local copies, waits for them, and re-layouts, per_device(): lax.optimization_barrier((up, down, features, green_kernel))  7.73 us
    pallas_call x1, Pallas kernels, per_device(): pl.pallas_call(tail_kernel, in_specs=[VMEM] * 9, out_specs=VMEM, out_shap...  7.12 us
    pallas_call x1, Pallas kernels, per_device(): pl.pallas_call(first_own_kernel, in_specs=[VMEM] * 4, out_specs=VMEM, out...  6.14 us
    all_to_all x1, starting transfers between devices, per_device(): everyone = lax.all_to_all(payload, axes, 0, 0, tiled=True)  5.82 us
  transfers between devices with their start and end apart: 6, of which 1 were waited for; matrix products, arithmetic and copies ran while one was open for 10% of the time, Pallas kernels for 55%

profile of v3, /device:TPU:0, one launch (start us, length us, event | category | flops | bytes accessed | tf_op | source)
XLA Modules:
  0.0 93.2 jit_solution(1082917314855009825)
XLA Ops:
  0.0 3.1 %shard_map.154 = (f32[200,512]{1,0:T(8,128)}, f32[200,512]{1,0:T(8,128)}, f32[32,24,128]{2,1,0:T(8,128)}) custom-call(f32[512,512]{1,0:T(8,128)} %features_ref.3, f32[3,512]{1,0:T(4,128)} %places_ref.9, f32[2,512]{1,0:T(2,128)} %bitcast.7, s32[3,8]{1,0:T(4,128)} %anchor_ref.1, s32[1,2,3]{2,1,0:T(2,128)} %exports_ref.3, s32[1,2]{1,0:T(1,128)} %counts_ref.1), custom_call_target="tpu_custom_call" | custom-call | tf_op jit(solution)/shard_map/pallas_call | solution.py:739
  3.1 2.9 %collective-permute-start = (f32[200,512]{1,0:T(8,128)}, f32[200,512]{1,0:T(8,128)S(1)}, u32[]{:S(2)}, u32[]{:S(2)}) collective-permute-start(f32[200,512]{1,0:T(8,128)} %get-tuple-element.34), channel_id=1, source_target_pairs={{0,1},{1,2},{2,3},{3,4},{4,5},{5,6},{6,7},{7,8},{8,9},{9,10},{10,1... | collective-permute-start | bytes 1228808 | tf_op jit(solution)/shard_map/ppermute | solution.py:737
  6.0 3.4 %collective-permute-start.1 = (f32[200,512]{1,0:T(8,128)}, f32[200,512]{1,0:T(8,128)S(1)}, u32[]{:S(2)}, u32[]{:S(2)}) collective-permute-start(f32[200,512]{1,0:T(8,128)} %get-tuple-element.35), channel_id=1, source_target_pairs={{0,31},{1,0},{2,1},{3,2},{4,3},{5,4},{6,5},{7,6},{8,7},{9,8},{10,9... | collective-permute-start | bytes 1228808 | tf_op jit(solution)/shard_map/ppermute | solution.py:737
  9.5 7.7 %copy.17 = f32[96,2,2,192,12]{0,3,2,1,4:T(8,128)} copy(f32[96,2,2,192,12]{3,2,4,1,0:T(2,128)} %param.26) | data formatting | bytes 7077888 | tf_op jit(solution)/shard_map/optimization_barrier | solution.py:750
  17.2 6.1 %shard_map.155.own_ref = f32[512,512]{1,0:T(8,128)} custom-call(f32[512,512]{1,0:T(8,128)} %features_ref.3, f32[3,512]{1,0:T(4,128)} %places_ref.9, f32[512,512]{1,0:T(8,128)} %value_one_ref.3, f32[8,512]{1,0:T(8,128)} %weight_ref.5), custom_call_target="tpu_custom_call" | custom-call | tf_op jit(solution)/shard_map/pallas_call | solution.py:753
  23.3 0.0 collective-permute-done.up_ref
  23.3 0.0 copy-start.2
  23.3 1.1 %collective-permute-done.1.down_ref = f32[200,512]{1,0:T(8,128)S(1)} collective-permute-done((f32[200,512]{1,0:T(8,128)}, f32[200,512]{1,0:T(8,128)S(1)}, u32[]{:S(2)}, u32[]{:S(2)}) %collective-permute-start.1) | collective-permute-done | bytes 409632 | tf_op jit(solution)/shard_map/ppermute | solution.py:737
  24.4 0.0 copy-start.3
  24.4 5.8 %all-to-all-start = ((f32[32,24,128]{2,1,0:T(8,128)}), f32[32,24,128]{2,1,0:T(8,128)S(1)}, u32[]{:S(2)}, u32[]{:S(2)}) async-start(f32[32,24,128]{2,1,0:T(8,128)} %get-tuple-element.36), calls=%async_computation | async-start | bytes 786432 | tf_op jit(solution)/shard_map/all_to_all | solution.py:763
  30.3 0.0 copy-done.2
  30.3 0.0 copy-done.3
  30.3 12.3 %shard_map.156 = (f32[512,512]{1,0:T(8,128)}, f32[512,512]{1,0:T(8,128)}, f32[192,512]{1,0:T(8,128)}, f32[192,512]{1,0:T(8,128)}, f32[8,512]{1,0:T(8,128)}) custom-call(f32[512,512]{1,0:T(8,128)} %features_ref.3, f32[512,512]{1,0:T(8,128)} %shard_map.155.own_ref, f32[200,512]{1,0:T(8,128)} %copy-done.2, f32[200,512]{1,0:T(8,128)} %copy-done.3, ...), custom_call_target="tpu_custom_call" | custom-call | tf_op jit(solution)/shard_map/pallas_call | solution.py:765
  42.6 1.8 %collective-permute-start.2 = (f32[192,512]{1,0:T(8,128)}, f32[192,512]{1,0:T(8,128)S(1)}, u32[]{:S(2)}, u32[]{:S(2)}) collective-permute-start(f32[192,512]{1,0:T(8,128)} %get-tuple-element.43), channel_id=1, source_target_pairs={{0,1},{1,2},{2,3},{3,4},{4,5},{5,6},{6,7},{7,8},{8,9},{9,10},{10,1... | collective-permute-start | bytes 1179656 | tf_op jit(solution)/shard_map/ppermute | solution.py:737
  44.4 3.7 %collective-permute-start.3 = (f32[192,512]{1,0:T(8,128)}, f32[192,512]{1,0:T(8,128)S(1)}, u32[]{:S(2)}, u32[]{:S(2)}) collective-permute-start(f32[192,512]{1,0:T(8,128)} %get-tuple-element.44), channel_id=1, source_target_pairs={{0,31},{1,0},{2,1},{3,2},{4,3},{5,4},{6,5},{7,6},{8,7},{9,8},{10,9... | collective-permute-start | bytes 1179656 | tf_op jit(solution)/shard_map/ppermute | solution.py:737
  48.1 0.6 pad_add_fusion.place_ref
  48.7 0.0 all-to-all-done.payload_ref
  48.7 0.0 copy-start
  48.7 0.7 slice_convert_fusion
  49.4 0.1 copy-done
  49.4 21.8 %shard_map.157 = f32[32,16,128]{2,1,0:T(8,128)} custom-call(s32[3]{0:T(128)} %pad_add_fusion.place_ref, s32[32,8]{1,0:T(8,128)} %bitcast.6, f32[32,24,128]{2,1,0:T(8,128)} %copy-done, f32[12,2,2,192,96]{4,3,2,1,0:T(8,128)} %bitcast.5, bf16[192,576]{1,0:T(8,128)(2,1)} %constant.14.clone.forward_ref, bf16[192,576]{1,0:T(8,128)(2,1)} %constant.15.clone.back_ref), custom_call_target="tpu_custom_call" | custom-call | tf_op jit(solution)/shard_map/pallas_call | solution.py:789
  71.3 0.0 collective-permute-done.2.up_two_ref
  71.3 0.0 copy-start.4
  71.3 0.0 collective-permute-done.3.down_two_ref
  71.3 0.0 copy-start.5
  71.3 2.8 %all-to-all-start.1 = ((f32[32,16,128]{2,1,0:T(8,128)}), f32[32,16,128]{2,1,0:T(8,128)S(1)}, u32[]{:S(2)}, u32[]{:S(2)}) async-start(f32[32,16,128]{2,1,0:T(8,128)} %shard_map.157), calls=%async_computation.1 | async-start | bytes 524288 | tf_op jit(solution)/shard_map/all_to_all | solution.py:794
  74.1 0.0 copy-done.4
  74.1 0.0 copy-done.5
  74.2 11.2 %shard_map.158 = (f32[512,512]{1,0:T(8,128)}, f32[8,512]{1,0:T(8,128)}) custom-call(f32[512,512]{1,0:T(8,128)} %get-tuple-element.46.values_ref, f32[192,512]{1,0:T(8,128)} %copy-done.4, f32[192,512]{1,0:T(8,128)} %copy-done.5, f32[8,512]{1,0:T(8,128)} %get-tuple-element.49.ghost_places_ref, f32[3,512]{1,0:T(4,128)} %places_ref.9, f32[8,512]{1,0:T(8,128)} %weight_ref.7, ...), custom_call_target="tpu_custom_call" | custom-call | tf_op jit(solution)/shard_map/pallas_call | solution.py:796
  85.4 0.0 all-to-all-done.1.received_ref
  85.4 0.0 copy-start.1
  85.4 0.7 copy-done.1
  86.1 7.1 %shard_map.159 = f32[512,512]{1,0:T(8,128)} custom-call(f32[32,16,128]{2,1,0:T(8,128)} %copy-done.1, f32[512,512]{1,0:T(8,128)} %get-tuple-element.50.messages_ref, f32[512,512]{1,0:T(8,128)} %get-tuple-element.51.hidden_ref, f32[8,512]{1,0:T(8,128)} %get-tuple-element.49.ghost_places_ref, f32[3,512]{1,0:T(4,128)} %places_ref.9, f32[8,512]{1,0:T(8,128)} %weight_ref.7, ...), custom_call_target="tpu_custom_call" | custom-call | tf_op jit(solution)/shard_map/pallas_call | solution.py:805
Async XLA Ops:
  3.1 20.3 %collective-permute-start = (f32[200,512]{1,0:T(8,128)}, f32[200,512]{1,0:T(8,128)S(1)}, u32[]{:S(2)}, u32[]{:S(2)}) collective-permute-start(f32[200,512]{1,0:T(8,128)} %get-tuple-element.34), channel_id=1, source_target_pairs={{0,1},{1,2},{2,3},{3,4},{4,5},{5,6},{6,7},{7,8},{8,9},{9,10},{10,1... | collective-permute-start | bytes 1228808 | tf_op jit(solution)/shard_map/ppermute | solution.py:737
  6.0 18.4 %collective-permute-start.1 = (f32[200,512]{1,0:T(8,128)}, f32[200,512]{1,0:T(8,128)S(1)}, u32[]{:S(2)}, u32[]{:S(2)}) collective-permute-start(f32[200,512]{1,0:T(8,128)} %get-tuple-element.35), channel_id=1, source_target_pairs={{0,31},{1,0},{2,1},{3,2},{4,3},{5,4},{6,5},{7,6},{8,7},{9,8},{10,9... | collective-permute-start | bytes 1228808 | tf_op jit(solution)/shard_map/ppermute | solution.py:737
  23.3 6.9 %copy-start.2 = (f32[200,512]{1,0:T(8,128)}, f32[200,512]{1,0:T(8,128)S(1)}, u32[]{:S(2)}) copy-start(f32[200,512]{1,0:T(8,128)S(1)} %collective-permute-done.up_ref) | copy-start | bytes 1228804
  24.4 5.8 %copy-start.3 = (f32[200,512]{1,0:T(8,128)}, f32[200,512]{1,0:T(8,128)S(1)}, u32[]{:S(2)}) copy-start(f32[200,512]{1,0:T(8,128)S(1)} %collective-permute-done.1.down_ref) | copy-start | bytes 1228804
  24.4 24.3 %all-to-all-start = ((f32[32,24,128]{2,1,0:T(8,128)}), f32[32,24,128]{2,1,0:T(8,128)S(1)}, u32[]{:S(2)}, u32[]{:S(2)}) async-start(f32[32,24,128]{2,1,0:T(8,128)} %get-tuple-element.36), calls=%async_computation | async-start | bytes 786432 | tf_op jit(solution)/shard_map/all_to_all | solution.py:763
  42.6 28.7 %collective-permute-start.2 = (f32[192,512]{1,0:T(8,128)}, f32[192,512]{1,0:T(8,128)S(1)}, u32[]{:S(2)}, u32[]{:S(2)}) collective-permute-start(f32[192,512]{1,0:T(8,128)} %get-tuple-element.43), channel_id=1, source_target_pairs={{0,1},{1,2},{2,3},{3,4},{4,5},{5,6},{6,7},{7,8},{8,9},{9,10},{10,1... | collective-permute-start | bytes 1179656 | tf_op jit(solution)/shard_map/ppermute | solution.py:737
  44.4 26.9 %collective-permute-start.3 = (f32[192,512]{1,0:T(8,128)}, f32[192,512]{1,0:T(8,128)S(1)}, u32[]{:S(2)}, u32[]{:S(2)}) collective-permute-start(f32[192,512]{1,0:T(8,128)} %get-tuple-element.44), channel_id=1, source_target_pairs={{0,31},{1,0},{2,1},{3,2},{4,3},{5,4},{6,5},{7,6},{8,7},{9,8},{10,9... | collective-permute-start | bytes 1179656 | tf_op jit(solution)/shard_map/ppermute | solution.py:737
  48.7 0.8 copy-start
  71.3 2.9 %copy-start.4 = (f32[192,512]{1,0:T(8,128)}, f32[192,512]{1,0:T(8,128)S(1)}, u32[]{:S(2)}) copy-start(f32[192,512]{1,0:T(8,128)S(1)} %collective-permute-done.2.up_two_ref) | copy-start | bytes 1179652
  71.3 2.9 %copy-start.5 = (f32[192,512]{1,0:T(8,128)}, f32[192,512]{1,0:T(8,128)S(1)}, u32[]{:S(2)}) copy-start(f32[192,512]{1,0:T(8,128)S(1)} %collective-permute-done.3.down_two_ref) | copy-start | bytes 1179652
  71.3 14.1 %all-to-all-start.1 = ((f32[32,16,128]{2,1,0:T(8,128)}), f32[32,16,128]{2,1,0:T(8,128)S(1)}, u32[]{:S(2)}, u32[]{:S(2)}) async-start(f32[32,16,128]{2,1,0:T(8,128)} %shard_map.157), calls=%async_computation.1 | async-start | bytes 524288 | tf_op jit(solution)/shard_map/all_to_all | solution.py:794
  85.4 0.7 copy-start.1

commit v4 on v3

--- a/solution.py
+++ b/solution.py
@@ -172,7 +172,7 @@
     return jnp.transpose(jnp.concatenate([places_ref[...], jnp.zeros((5, atoms), f32)], axis=0))
 
 
-def ghost_messages(ghost_values_ref, places_ref, ghost_places, weight_ref, out_ref):
+def ghost_messages(ghost_values_ref, places_ref, ghost_places, weight_ref):
     weights = scaled_weights(weight_ref)
     ghosts = 2 * NH * BA
     near, ratio = pair_terms(
@@ -191,13 +191,14 @@
             jnp.concatenate([values * weights[k], values * weights[k + 1]], axis=0)
         )
 
-    total = out_ref[...]
+    total = None
     ready = operands(0)
     for k in range(0, NR, 2):
         following = operands(k + 2) if k + 2 < NR else None
-        total = total + product(*ready)
+        part = product(*ready)
+        total = part if total is None else total + part
         ready = following
-    out_ref[...] = total
+    return total
 
 
 def own_messages(values_ref, places_ref, weight_ref, out_ref):
@@ -241,24 +242,48 @@
     return hidden + product(split(active), split(output_ref[...]))
 
 
-def first_own_kernel(features_ref, places_ref, value_one_ref, weight_ref, messages_ref, values):
+def first_own_kernel(
+    features_ref, places_ref, value_one_ref, weight_ref, return_ref, value_two_ref,
+    messages_ref, returned_ref,
+    values,
+):
     values[...] = product(split(features_ref[...]), split(value_one_ref[...]))
     own_messages(values, places_ref, weight_ref, messages_ref)
+    return_rows = jnp.concatenate(
+        [return_ref[...], jnp.zeros((6, return_ref.shape[1]), f32)], axis=0
+    )
+    returned_ref[...] = product(split(return_rows), split(value_two_ref[...]))
+
+
+def fetched(sources, targets, arrived):
+    copies = [
+        pltpu.make_async_copy(source, target, arrived.at[n])
+        for n, (source, target) in enumerate(zip(sources, targets))
+    ]
+    for copy in copies:
+        copy.start()
+    return copies
 
 
 def first_layer_kernel(
-    features_ref, own_ref, up_ref, down_ref, places_ref, value_one_ref, output_one_ref, weight_ref,
-    value_two_ref, exports_ref,
+    up_ref, down_ref, places_ref, value_one_ref, weight_ref, exports_ref,
+    features_hbm, own_hbm, output_one_hbm, value_two_hbm,
     hidden_ref, values_two_ref, up_two_ref, down_two_ref, ghost_places_ref,
-    ghost_values, messages,
+    ghost_values, features_ref, own_ref, output_one_ref, value_two_ref, arrived,
 ):
+    copies = fetched(
+        (features_hbm, own_hbm, output_one_hbm, value_two_hbm),
+        (features_ref, own_ref, output_one_ref, value_two_ref),
+        arrived,
+    )
     base = NH * BA
     ghost_rows = jnp.concatenate([up_ref[:base, :], down_ref[:base, :]], axis=0)
     ghost_values[...] = product(split(ghost_rows), split(value_one_ref[...]))
     ghost_places_ref[...] = up_ref[base : base + 8, :] + down_ref[base : base + 8, :]
-    messages[...] = own_ref[...]
-    ghost_messages(ghost_values, places_ref, ghost_places_ref[...], weight_ref, messages)
-    hidden_ref[...] = finish(features_ref[...], messages[...], output_one_ref)
+    messages = ghost_messages(ghost_values, places_ref, ghost_places_ref[...], weight_ref)
+    for copy in copies:
+        copy.wait()
+    hidden_ref[...] = finish(features_ref[...], own_ref[...] + messages, output_one_ref)
     values_two_ref[...] = product(split(hidden_ref[...]), split(value_two_ref[...]))
     pack_rows(up_two_ref, values_two_ref, exports_ref, 0)
     pack_rows(down_two_ref, values_two_ref, exports_ref, 1)
@@ -266,26 +291,29 @@
 
 def second_layer_kernel(
     values_ref, up_two_ref, down_two_ref, ghost_places_ref, places_ref, weight_ref,
-    return_ref, value_two_ref,
-    messages_ref, returned_ref,
+    messages_ref,
     ghost_values,
 ):
     base = NH * BA
     ghost_values[:base, :] = up_two_ref[...]
     ghost_values[base:, :] = down_two_ref[...]
     own_messages(values_ref, places_ref, weight_ref, messages_ref)
-    ghost_messages(ghost_values, places_ref, ghost_places_ref[...], weight_ref, messages_ref)
-    return_rows = jnp.concatenate(
-        [return_ref[...], jnp.zeros((6, return_ref.shape[1]), f32)], axis=0
-    )
-    returned_ref[...] = product(split(return_rows), split(value_two_ref[...]))
+    messages_ref[...] += ghost_messages(
+        ghost_values, places_ref, ghost_places_ref[...], weight_ref
+    )
 
 
 def tail_kernel(
-    received_ref, messages_ref, hidden_ref, ghost_places_ref, places_ref, weight_ref,
-    return_ref, returned_ref, output_two_ref,
+    received_ref, ghost_places_ref, places_ref, weight_ref, return_ref, returned_ref,
+    messages_hbm, hidden_hbm, output_two_hbm,
     updated_ref,
+    messages_ref, hidden_ref, output_two_ref, arrived,
 ):
+    copies = fetched(
+        (messages_hbm, hidden_hbm, output_two_hbm),
+        (messages_ref, hidden_ref, output_two_ref),
+        arrived,
+    )
     atoms = hidden_ref.shape[0]
     ghosts = 2 * NH * BA
     potentials = jnp.sum(received_ref[...], axis=0)
@@ -327,13 +355,20 @@
             jnp.concatenate([near * ghost_potential[c], own_near * own_potential[c]], axis=0)
             for c in range(2)
         ]
-        sums = []
-        for k in range(NR):
+        sums = [None] * (2 * NR)
+        for start in range(0, ratio.shape[0], 8):
+            tile = slice(start, start + 8)
+            step = ratio[tile]
             for c in range(2):
-                sums.append(jnp.sum(terms[c], axis=0, keepdims=True))
-                if k + 1 < NR:
-                    terms[c] = terms[c] * ratio
-        pieces.append(jnp.concatenate(sums, axis=0))
+                term = terms[c][tile]
+                for k in range(NR):
+                    at = 2 * k + c
+                    sums[at] = term if sums[at] is None else sums[at] + term
+                    if k + 1 < NR:
+                        term = term * step
+        pieces.append(
+            jnp.concatenate([jnp.sum(total, axis=0, keepdims=True) for total in sums], axis=0)
+        )
     gathered = jnp.transpose(jnp.concatenate(pieces, axis=1))
     spread = jnp.concatenate(
         [
@@ -343,6 +378,8 @@
         ],
         axis=0,
     )
+    for copy in copies:
+        copy.wait()
     messages = messages_ref[...] + narrow_product(split(gathered), split(spread))
     back = [return_ref[c : c + 1, :] for c in range(2)]
     layer_input = jnp.concatenate(
@@ -375,7 +412,7 @@
 
 def reciprocal_kernel(
     grid, slabs, per_slab, second, depth,
-    place_ref, exports_ref, payload_ref, green_hbm, forward_ref, back_ref,
+    exports_ref, payload_ref, green_hbm, forward_ref, back_ref,
     out_ref,
     green_ref, green_arrived, planes_real, planes_imag, turns_high, turns_low, brick, carry,
     shift_cos, shift_sin, stage_cos, stage_sin, chosen, potential,
@@ -394,8 +431,8 @@
     chunks = atoms // LANES
     own = NB * BA // LANES
     wide = depth
-    first_v = (place_ref[0] * second).astype(f32)
-    first_w = (place_ref[1] * place_ref[2]).astype(f32)
+    first_v = (lax.axis_index("dom") * second).astype(f32)
+    first_w = (lax.axis_index("rec") * green_hbm.shape[4]).astype(f32)
     period = float(grid)
 
     row = rows_iota((rows, 1))
@@ -677,7 +714,7 @@
     sides = 2 * pairs_of(slabs, per_slab)
     return pl.pallas_call(
         functools.partial(reciprocal_kernel, grid, slabs, per_slab, second, depth),
-        in_specs=[SMEM, SMEM, VMEM, pl.BlockSpec(memory_space=pl.ANY), VMEM, VMEM],
+        in_specs=[SMEM, VMEM, ANY, VMEM, VMEM],
         out_specs=VMEM,
         out_shape=jax.ShapeDtypeStruct((domains, 16, LANES), f32),
         scratch_shapes=[
@@ -702,6 +739,7 @@
 
 VMEM = pl.BlockSpec(memory_space=pltpu.VMEM)
 SMEM = pl.BlockSpec(memory_space=pltpu.SMEM)
+ANY = pl.BlockSpec(memory_space=pl.ANY)
 
 
 def per_device(
@@ -750,21 +788,21 @@
     up, down, features, green_kernel = lax.optimization_barrier((up, down, features, green_kernel))
     up = around(up, 1)
     down = around(down, -1)
-    own = pl.pallas_call(
+    own, returned = pl.pallas_call(
         first_own_kernel,
-        in_specs=[VMEM] * 4,
-        out_specs=VMEM,
-        out_shape=shape(atoms, width),
+        in_specs=[VMEM] * 6,
+        out_specs=[VMEM] * 2,
+        out_shape=[shape(atoms, width), shape(8, width)],
         scratch_shapes=[pltpu.VMEM((atoms, width), f32)],
         compiler_params=params(),
-    )(features, positions, value_one, radial_one)
+    )(features, positions, value_one, radial_one, return_weight, value_two)
     green = jnp.transpose(green_kernel, (4, 1, 2, 3, 0))
     payload, own, green, up, down = lax.optimization_barrier((payload, own, green, up, down))
     everyone = lax.all_to_all(payload, axes, 0, 0, tiled=True)
 
     hidden, values_two, up_two, down_two, ghost_places = pl.pallas_call(
         first_layer_kernel,
-        in_specs=[VMEM] * 9 + [SMEM],
+        in_specs=[VMEM] * 5 + [SMEM] + [ANY] * 4,
         out_specs=[VMEM] * 5,
         out_shape=[
             shape(atoms, width), shape(atoms, width), shape(base, width), shape(base, width),
@@ -773,43 +811,51 @@
         scratch_shapes=[
             pltpu.VMEM((2 * base, width), f32),
             pltpu.VMEM((atoms, width), f32),
+            pltpu.VMEM((atoms, width), f32),
+            pltpu.VMEM((width, width), f32),
+            pltpu.VMEM((width, width), f32),
+            pltpu.SemaphoreType.DMA((4,)),
         ],
         compiler_params=params(),
-    )(features, own, up, down, positions, value_one, output_one, radial_one, value_two, exports)
+    )(up, down, positions, value_one, radial_one, exports, features, own, output_one, value_two)
 
     everyone, hidden = lax.optimization_barrier((everyone, hidden))
     up_two = around(up_two, 1)
     down_two = around(down_two, -1)
 
-    place = jnp.stack(
-        [lax.axis_index("dom"), lax.axis_index("rec"), jnp.int32(depth_rows)]
-    ).astype(jnp.int32)
     all_exports = everyone[:, 5 * chunks + 3, :8].astype(jnp.int32)
     table, table_back = transform_tables(grid)
     outgoing = build_reciprocal(grid, slabs, per_slab, second, depth, depth_rows)(
-        place, all_exports, everyone, green, table, table_back
+        all_exports, everyone, green, table, table_back
     )
 
     outgoing, up_two, down_two = lax.optimization_barrier((outgoing, up_two, down_two))
     received = lax.all_to_all(outgoing, axes, 0, 0, tiled=True)
 
-    messages, returned = pl.pallas_call(
+    messages = pl.pallas_call(
         second_layer_kernel,
-        in_specs=[VMEM] * 8,
-        out_specs=[VMEM] * 2,
-        out_shape=[shape(atoms, width), shape(8, width)],
+        in_specs=[VMEM] * 6,
+        out_specs=VMEM,
+        out_shape=shape(atoms, width),
         scratch_shapes=[pltpu.VMEM((2 * base, width), f32)],
         compiler_params=params(),
-    )(values_two, up_two, down_two, ghost_places, positions, radial_two, return_weight, value_two)
+    )(values_two, up_two, down_two, ghost_places, positions, radial_two)
 
     return pl.pallas_call(
         tail_kernel,
-        in_specs=[VMEM] * 9,
+        in_specs=[VMEM] * 6 + [ANY] * 3,
         out_specs=VMEM,
         out_shape=shape(atoms, width),
+        scratch_shapes=[
+            pltpu.VMEM((atoms, width), f32),
+            pltpu.VMEM((atoms, width), f32),
+            pltpu.VMEM((width, width), f32),
+            pltpu.SemaphoreType.DMA((3,)),
+        ],
         compiler_params=params(),
     )(
-        received, messages, hidden, ghost_places, positions, radial_two, return_weight, returned, output_two
+        received, ghost_places, positions, radial_two, return_weight, returned,
+        messages, hidden, output_two,
     )
 
 

time: 93.8 us -> 90.8 us (0.968)
  Pallas kernels: 61.7 us -> 59.4 us
    pallas_call x4, Pallas kernels: 36.8 us -> 34.5 us  [the longest x1 11.2 us: per_device(): pl.pallas_call(first_layer_kernel, in_specs=[VMEM] * 5 + [SMEM] + [ANY] *...]
  transfers between devices with their start and end apart: 6 -> 6, of which waited for: 1 -> 1; matrix products, arithmetic and copies ran while one was open for 10% -> 9% of each run, Pallas kernels for 55% -> 56%
where the time goes in v4:
time: 90.8 us; the launch traced here: 90.2 us
  Pallas kernels  59.4 us (65%)
  starting transfers between devices  20.6 us (23%)
  local copies, waits for them, and re-layouts  8.55 us (9%)
    pallas_call x1, Pallas kernels, per_device(): build_reciprocal(grid, slabs, per_slab, second, depth, depth_rows)  21.8 us
    ppermute x4, starting transfers between devices, around(): lax.ppermute(rows, axes, [(i, (i + by) % domains) for i in range(domains)])  11.9 us
    pallas_call x1, Pallas kernels, per_device(): pl.pallas_call(first_layer_kernel, in_specs=[VMEM] * 5 + [SMEM] + [ANY] *...  11.2 us
    pallas_call x1, Pallas kernels, per_device(): pl.pallas_call(second_layer_kernel, in_specs=[VMEM] * 6, out_specs=VMEM,...  10.9 us
    optimization_barrier x1, local copies, waits for them, and re-layouts, per_device(): lax.optimization_barrier((up, down, features, green_kernel))  7.73 us
    pallas_call x1, Pallas kernels, per_device(): pl.pallas_call(first_own_kernel, in_specs=[VMEM] * 6, out_specs=[VMEM] *...  6.51 us
    pallas_call x1, Pallas kernels, per_device(): pl.pallas_call(tail_kernel, in_specs=[VMEM] * 6 + [ANY] * 3, out_specs=VM...  5.99 us
    all_to_all x1, starting transfers between devices, per_device(): everyone = lax.all_to_all(payload, axes, 0, 0, tiled=True)  5.82 us
  transfers between devices with their start and end apart: 6, of which 1 were waited for; matrix products, arithmetic and copies ran while one was open for 9% of the time, Pallas kernels for 56%

profile of v4, /device:TPU:0, one launch (start us, length us, event | category | flops | bytes accessed | tf_op | source)
XLA Modules:
  0.0 90.2 jit_solution(6780780975096841902)
XLA Ops:
  0.0 3.1 %shard_map.154 = (f32[200,512]{1,0:T(8,128)}, f32[200,512]{1,0:T(8,128)}, f32[32,24,128]{2,1,0:T(8,128)}) custom-call(f32[512,512]{1,0:T(8,128)} %features_hbm, f32[3,512]{1,0:T(4,128)} %places_ref.9, f32[2,512]{1,0:T(2,128)} %bitcast.5, s32[3,8]{1,0:T(4,128)} %anchor_ref.1, s32[1,2,3]{2,1,0:T(2,128)} %exports_ref.3, s32[1,2]{1,0:T(1,128)} %counts_ref.1), custom_call_target="tpu_custom_call" | custom-call | tf_op jit(solution)/shard_map/pallas_call | solution.py:777
  3.1 2.9 %collective-permute-start = (f32[200,512]{1,0:T(8,128)}, f32[200,512]{1,0:T(8,128)S(1)}, u32[]{:S(2)}, u32[]{:S(2)}) collective-permute-start(f32[200,512]{1,0:T(8,128)} %get-tuple-element.35), channel_id=1, source_target_pairs={{0,1},{1,2},{2,3},{3,4},{4,5},{5,6},{6,7},{7,8},{8,9},{9,10},{10,1... | collective-permute-start | bytes 1228808 | tf_op jit(solution)/shard_map/ppermute | solution.py:775
  6.0 3.4 %collective-permute-start.1 = (f32[200,512]{1,0:T(8,128)}, f32[200,512]{1,0:T(8,128)S(1)}, u32[]{:S(2)}, u32[]{:S(2)}) collective-permute-start(f32[200,512]{1,0:T(8,128)} %get-tuple-element.36), channel_id=1, source_target_pairs={{0,31},{1,0},{2,1},{3,2},{4,3},{5,4},{6,5},{7,6},{8,7},{9,8},{10,9... | collective-permute-start | bytes 1228808 | tf_op jit(solution)/shard_map/ppermute | solution.py:775
  9.5 7.7 %copy.17 = f32[96,2,2,192,12]{0,3,2,1,4:T(8,128)} copy(f32[96,2,2,192,12]{3,2,4,1,0:T(2,128)} %param.26) | data formatting | bytes 7077888 | tf_op jit(solution)/shard_map/optimization_barrier | solution.py:788
  17.2 6.5 %shard_map.155 = (f32[512,512]{1,0:T(8,128)}, f32[8,512]{1,0:T(8,128)}) custom-call(f32[512,512]{1,0:T(8,128)} %features_hbm, f32[3,512]{1,0:T(4,128)} %places_ref.9, f32[512,512]{1,0:T(8,128)} %value_one_ref.3, f32[8,512]{1,0:T(8,128)} %weight_ref.5, f32[2,512]{1,0:T(2,128)} %return_ref.3, f32[512,512]{1,0:T(8,128)} %value_two_hbm.1), custom_call_target="tpu_custom_call" | custom-call | tf_op jit(solution)/shard_map/pallas_call | solution.py:791
  23.7 0.0 collective-permute-done.up_ref
  23.7 0.0 copy-start.2
  23.7 0.7 collective-permute-done.1.down_ref
  24.4 0.0 copy-start.3
  24.4 5.8 %all-to-all-start = ((f32[32,24,128]{2,1,0:T(8,128)}), f32[32,24,128]{2,1,0:T(8,128)S(1)}, u32[]{:S(2)}, u32[]{:S(2)}) async-start(f32[32,24,128]{2,1,0:T(8,128)} %get-tuple-element.37), calls=%async_computation | async-start | bytes 786432 | tf_op jit(solution)/shard_map/all_to_all | solution.py:801
  30.3 0.0 copy-done.2
  30.3 0.0 copy-done.3
  30.3 11.2 %shard_map.156 = (f32[512,512]{1,0:T(8,128)}, f32[512,512]{1,0:T(8,128)}, f32[192,512]{1,0:T(8,128)}, f32[192,512]{1,0:T(8,128)}, f32[8,512]{1,0:T(8,128)}) custom-call(f32[200,512]{1,0:T(8,128)} %copy-done.2, f32[200,512]{1,0:T(8,128)} %copy-done.3, f32[3,512]{1,0:T(4,128)} %places_ref.9, f32[512,512]{1,0:T(8,128)} %value_one_ref.3, f32[8,512]{1,0:T(8,128)} %weight_ref.5, ...), custom_call_target="tpu_custom_call" | custom-call | tf_op jit(solution)/shard_map/pallas_call | solution.py:803
  41.4 1.8 %collective-permute-start.2 = (f32[192,512]{1,0:T(8,128)}, f32[192,512]{1,0:T(8,128)S(1)}, u32[]{:S(2)}, u32[]{:S(2)}) collective-permute-start(f32[192,512]{1,0:T(8,128)} %get-tuple-element.44), channel_id=1, source_target_pairs={{0,1},{1,2},{2,3},{3,4},{4,5},{5,6},{6,7},{7,8},{8,9},{9,10},{10,1... | collective-permute-start | bytes 1179656 | tf_op jit(solution)/shard_map/ppermute | solution.py:775
  43.3 3.7 %collective-permute-start.3 = (f32[192,512]{1,0:T(8,128)}, f32[192,512]{1,0:T(8,128)S(1)}, u32[]{:S(2)}, u32[]{:S(2)}) collective-permute-start(f32[192,512]{1,0:T(8,128)} %get-tuple-element.45), channel_id=1, source_target_pairs={{0,31},{1,0},{2,1},{3,2},{4,3},{5,4},{6,5},{7,6},{8,7},{9,8},{10,9... | collective-permute-start | bytes 1179656 | tf_op jit(solution)/shard_map/ppermute | solution.py:775
  47.0 0.0 all-to-all-done.payload_ref
  47.0 0.0 copy-start
  47.0 0.7 slice_convert_fusion
  47.7 0.1 copy-done
  47.7 21.8 %shard_map.157 = f32[32,16,128]{2,1,0:T(8,128)} custom-call(s32[32,8]{1,0:T(8,128)} %bitcast.4, f32[32,24,128]{2,1,0:T(8,128)} %copy-done, f32[12,2,2,192,96]{4,3,2,1,0:T(8,128)} %bitcast.3, bf16[192,576]{1,0:T(8,128)(2,1)} %constant.4.clone.forward_ref, bf16[192,576]{1,0:T(8,128)(2,1)} %constant.5.clone.back_ref), custom_call_target="tpu_custom_call" | custom-call | tf_op jit(solution)/shard_map/pallas_call | solution.py:828
  69.6 0.0 collective-permute-done.2.up_two_ref
  69.6 0.0 copy-start.4
  69.6 0.0 collective-permute-done.3.down_two_ref
  69.6 0.0 copy-start.5
  69.6 2.8 %all-to-all-start.1 = ((f32[32,16,128]{2,1,0:T(8,128)}), f32[32,16,128]{2,1,0:T(8,128)S(1)}, u32[]{:S(2)}, u32[]{:S(2)}) async-start(f32[32,16,128]{2,1,0:T(8,128)} %shard_map.157), calls=%async_computation.1 | async-start | bytes 524288 | tf_op jit(solution)/shard_map/all_to_all | solution.py:833
  72.5 0.0 copy-done.4
  72.5 0.0 copy-done.5
  72.5 10.9 %shard_map.158.messages_hbm = f32[512,512]{1,0:T(8,128)} custom-call(f32[512,512]{1,0:T(8,128)} %get-tuple-element.49.values_ref, f32[192,512]{1,0:T(8,128)} %copy-done.4, f32[192,512]{1,0:T(8,128)} %copy-done.5, f32[8,512]{1,0:T(8,128)} %get-tuple-element.47.ghost_places_ref, f32[3,512]{1,0:T(4,128)} %places_ref.9, f32[8,512]{1,0:T(8,128)} %weight_ref.7), custom_call_target="tpu_custom_call" | custom-call | tf_op jit(solution)/shard_map/pallas_call | solution.py:835
  83.3 0.0 all-to-all-done.1.received_ref
  83.3 0.0 copy-start.1
  83.3 0.7 copy-done.1
  84.1 6.0 %shard_map.159 = f32[512,512]{1,0:T(8,128)} custom-call(f32[32,16,128]{2,1,0:T(8,128)} %copy-done.1, f32[8,512]{1,0:T(8,128)} %get-tuple-element.47.ghost_places_ref, f32[3,512]{1,0:T(4,128)} %places_ref.9, f32[8,512]{1,0:T(8,128)} %weight_ref.7, f32[2,512]{1,0:T(2,128)} %return_ref.3, f32[8,512]{1,0:T(8,128)} %get-tuple-element.48.returned_ref, ...), custom_call_target="tpu_custom_call" | custom-call | tf_op jit(solution)/shard_map/pallas_call | solution.py:844
Async XLA Ops:
  3.1 20.6 %collective-permute-start = (f32[200,512]{1,0:T(8,128)}, f32[200,512]{1,0:T(8,128)S(1)}, u32[]{:S(2)}, u32[]{:S(2)}) collective-permute-start(f32[200,512]{1,0:T(8,128)} %get-tuple-element.35), channel_id=1, source_target_pairs={{0,1},{1,2},{2,3},{3,4},{4,5},{5,6},{6,7},{7,8},{8,9},{9,10},{10,1... | collective-permute-start | bytes 1228808 | tf_op jit(solution)/shard_map/ppermute | solution.py:775
  6.0 18.4 %collective-permute-start.1 = (f32[200,512]{1,0:T(8,128)}, f32[200,512]{1,0:T(8,128)S(1)}, u32[]{:S(2)}, u32[]{:S(2)}) collective-permute-start(f32[200,512]{1,0:T(8,128)} %get-tuple-element.36), channel_id=1, source_target_pairs={{0,31},{1,0},{2,1},{3,2},{4,3},{5,4},{6,5},{7,6},{8,7},{9,8},{10,9... | collective-permute-start | bytes 1228808 | tf_op jit(solution)/shard_map/ppermute | solution.py:775
  23.7 6.6 %copy-start.2 = (f32[200,512]{1,0:T(8,128)}, f32[200,512]{1,0:T(8,128)S(1)}, u32[]{:S(2)}) copy-start(f32[200,512]{1,0:T(8,128)S(1)} %collective-permute-done.up_ref) | copy-start | bytes 1228804
  24.4 5.8 %copy-start.3 = (f32[200,512]{1,0:T(8,128)}, f32[200,512]{1,0:T(8,128)S(1)}, u32[]{:S(2)}) copy-start(f32[200,512]{1,0:T(8,128)S(1)} %collective-permute-done.1.down_ref) | copy-start | bytes 1228804
  24.4 22.6 %all-to-all-start = ((f32[32,24,128]{2,1,0:T(8,128)}), f32[32,24,128]{2,1,0:T(8,128)S(1)}, u32[]{:S(2)}, u32[]{:S(2)}) async-start(f32[32,24,128]{2,1,0:T(8,128)} %get-tuple-element.37), calls=%async_computation | async-start | bytes 786432 | tf_op jit(solution)/shard_map/all_to_all | solution.py:801
  41.4 28.1 %collective-permute-start.2 = (f32[192,512]{1,0:T(8,128)}, f32[192,512]{1,0:T(8,128)S(1)}, u32[]{:S(2)}, u32[]{:S(2)}) collective-permute-start(f32[192,512]{1,0:T(8,128)} %get-tuple-element.44), channel_id=1, source_target_pairs={{0,1},{1,2},{2,3},{3,4},{4,5},{5,6},{6,7},{7,8},{8,9},{9,10},{10,1... | collective-permute-start | bytes 1179656 | tf_op jit(solution)/shard_map/ppermute | solution.py:775
  43.3 26.3 %collective-permute-start.3 = (f32[192,512]{1,0:T(8,128)}, f32[192,512]{1,0:T(8,128)S(1)}, u32[]{:S(2)}, u32[]{:S(2)}) collective-permute-start(f32[192,512]{1,0:T(8,128)} %get-tuple-element.45), channel_id=1, source_target_pairs={{0,31},{1,0},{2,1},{3,2},{4,3},{5,4},{6,5},{7,6},{8,7},{9,8},{10,9... | collective-permute-start | bytes 1179656 | tf_op jit(solution)/shard_map/ppermute | solution.py:775
  47.0 0.8 copy-start
  69.6 2.9 %copy-start.4 = (f32[192,512]{1,0:T(8,128)}, f32[192,512]{1,0:T(8,128)S(1)}, u32[]{:S(2)}) copy-start(f32[192,512]{1,0:T(8,128)S(1)} %collective-permute-done.2.up_two_ref) | copy-start | bytes 1179652
  69.6 2.9 %copy-start.5 = (f32[192,512]{1,0:T(8,128)}, f32[192,512]{1,0:T(8,128)S(1)}, u32[]{:S(2)}) copy-start(f32[192,512]{1,0:T(8,128)S(1)} %collective-permute-done.3.down_two_ref) | copy-start | bytes 1179652
  69.6 13.7 %all-to-all-start.1 = ((f32[32,16,128]{2,1,0:T(8,128)}), f32[32,16,128]{2,1,0:T(8,128)S(1)}, u32[]{:S(2)}, u32[]{:S(2)}) async-start(f32[32,16,128]{2,1,0:T(8,128)} %shard_map.157), calls=%async_computation.1 | async-start | bytes 524288 | tf_op jit(solution)/shard_map/all_to_all | solution.py:833
  83.3 0.7 copy-start.1

commit v5 on v4

--- a/solution.py
+++ b/solution.py
@@ -108,14 +108,15 @@
         out_ref[s * BA : (s + 1) * BA, :] = rows_ref[pl.ds(start, BA), :]
 
 
-def head_kernel(
-    features_ref, places_ref, charge_ref, anchor_ref, exports_ref, counts_ref,
-    up_ref, down_ref, payload_ref,
-    staged,
-):
+def pack_kernel(features_ref, places_ref, exports_ref, counts_ref, up_ref, down_ref):
     for out_ref, side in ((up_ref, 0), (down_ref, 1)):
         pack_rows(out_ref, features_ref, exports_ref, side)
         pack_places(out_ref, places_ref, exports_ref, counts_ref, side)
+
+
+def payload_kernel(
+    features_ref, places_ref, charge_ref, anchor_ref, exports_ref, payload_ref, staged
+):
     charge_rows = jnp.concatenate(
         [charge_ref[...], jnp.zeros((6, charge_ref.shape[1]), f32)], axis=0
     )
@@ -774,18 +775,23 @@
     def around(rows, by):
         return lax.ppermute(rows, axes, [(i, (i + by) % domains) for i in range(domains)])
 
-    up, down, payload = pl.pallas_call(
-        head_kernel,
-        in_specs=[VMEM] * 4 + [SMEM] * 2,
-        out_specs=[VMEM] * 3,
-        out_shape=[
-            shape(base + 8, width), shape(base + 8, width), shape(domains, payload_rows, LANES)
-        ],
+    up, down = pl.pallas_call(
+        pack_kernel,
+        in_specs=[VMEM] * 2 + [SMEM] * 2,
+        out_specs=[VMEM] * 2,
+        out_shape=[shape(base + 8, width), shape(base + 8, width)],
+        compiler_params=params(),
+    )(features, positions, exports, export_counts)
+
+    up, down, features, green_kernel = lax.optimization_barrier((up, down, features, green_kernel))
+    payload = pl.pallas_call(
+        payload_kernel,
+        in_specs=[VMEM] * 4 + [SMEM],
+        out_specs=VMEM,
+        out_shape=shape(domains, payload_rows, LANES),
         scratch_shapes=[pltpu.VMEM((payload_rows, LANES), f32)],
         compiler_params=params(),
-    )(features, positions, charge_weight.T, brick_anchor, exports, export_counts)
-
-    up, down, features, green_kernel = lax.optimization_barrier((up, down, features, green_kernel))
+    )(features, positions, charge_weight.T, brick_anchor, exports)
     up = around(up, 1)
     down = around(down, -1)
     own, returned = pl.pallas_call(

time: 90.8 us -> 90.5 us (level)
  Pallas kernels: 59.4 us -> 61.8 us
  starting transfers between devices: 20.6 us -> 18.6 us
    pallas_call x1 -> x2, Pallas kernels: 3.08 us -> 5.41 us  [the longest x1 2.73 us: per_device(): pl.pallas_call(pack_kernel, in_specs=[VMEM] * 2 + [SMEM] * 2, out_specs=[...]
    all_to_all x1, starting transfers between devices: 5.82 us -> 3.84 us  [per_device(): everyone = lax.all_to_all(payload, axes, 0, 0, tiled=True)]
  transfers between devices with their start and end apart: 6 -> 6, of which waited for: 1 -> 0; matrix products, arithmetic and copies ran while one was open for 9% -> 9% of each run, Pallas kernels for 56% -> 59%
where the time goes in v5:
time: 90.5 us; the launch traced here: 89.9 us
  Pallas kernels  61.8 us (68%)
  starting transfers between devices  18.6 us (21%)
  local copies, waits for them, and re-layouts  8.55 us (9%)
    pallas_call x1, Pallas kernels, per_device(): build_reciprocal(grid, slabs, per_slab, second, depth, depth_rows)  21.8 us
    ppermute x4, starting transfers between devices, around(): lax.ppermute(rows, axes, [(i, (i + by) % domains) for i in range(domains)])  11.9 us
    pallas_call x1, Pallas kernels, per_device(): pl.pallas_call(first_layer_kernel, in_specs=[VMEM] * 5 + [SMEM] + [ANY] *...  11.2 us
    pallas_call x1, Pallas kernels, per_device(): pl.pallas_call(second_layer_kernel, in_specs=[VMEM] * 6, out_specs=VMEM,...  10.9 us
    optimization_barrier x1, local copies, waits for them, and re-layouts, per_device(): lax.optimization_barrier((up, down, features, green_kernel))  7.73 us
    pallas_call x1, Pallas kernels, per_device(): pl.pallas_call(first_own_kernel, in_specs=[VMEM] * 6, out_specs=[VMEM] *...  6.51 us
    pallas_call x1, Pallas kernels, per_device(): pl.pallas_call(tail_kernel, in_specs=[VMEM] * 6 + [ANY] * 3, out_specs=VM...  5.99 us
    all_to_all x1, starting transfers between devices, per_device(): everyone = lax.all_to_all(payload, axes, 0, 0, tiled=True)  3.84 us
  transfers between devices with their start and end apart: 6, of which 0 were waited for; matrix products, arithmetic and copies ran while one was open for 9% of the time, Pallas kernels for 59%

profile of v5, /device:TPU:0, one launch (start us, length us, event | category | flops | bytes accessed | tf_op | source)
XLA Modules:
  0.0 89.9 jit_solution(6747792520809354725)
XLA Ops:
  0.0 2.7 %shard_map.154 = (f32[200,512]{1,0:T(8,128)}, f32[200,512]{1,0:T(8,128)}) custom-call(f32[512,512]{1,0:T(8,128)} %features_hbm, f32[3,512]{1,0:T(4,128)} %places_ref.11, s32[1,2,3]{2,1,0:T(2,128)} %exports_ref.5, s32[1,2]{1,0:T(1,128)} %counts_ref.1), custom_call_target="tpu_custom_call" | custom-call | tf_op jit(solution)/shard_map/pallas_call | solution.py:778
  2.7 2.9 %collective-permute-start = (f32[200,512]{1,0:T(8,128)}, f32[200,512]{1,0:T(8,128)S(1)}, u32[]{:S(2)}, u32[]{:S(2)}) collective-permute-start(f32[200,512]{1,0:T(8,128)} %get-tuple-element.33), channel_id=1, source_target_pairs={{0,1},{1,2},{2,3},{3,4},{4,5},{5,6},{6,7},{7,8},{8,9},{9,10},{10,1... | collective-permute-start | bytes 1228808 | tf_op jit(solution)/shard_map/ppermute | solution.py:776
  5.7 3.4 %collective-permute-start.1 = (f32[200,512]{1,0:T(8,128)}, f32[200,512]{1,0:T(8,128)S(1)}, u32[]{:S(2)}, u32[]{:S(2)}) collective-permute-start(f32[200,512]{1,0:T(8,128)} %get-tuple-element.34), channel_id=1, source_target_pairs={{0,31},{1,0},{2,1},{3,2},{4,3},{5,4},{6,5},{7,6},{8,7},{9,8},{10,9... | collective-permute-start | bytes 1228808 | tf_op jit(solution)/shard_map/ppermute | solution.py:776
  9.1 7.7 %copy.17 = f32[96,2,2,192,12]{0,3,2,1,4:T(8,128)} copy(f32[96,2,2,192,12]{3,2,4,1,0:T(2,128)} %param.26) | data formatting | bytes 7077888 | tf_op jit(solution)/shard_map/optimization_barrier | solution.py:786
  16.8 2.7 %shard_map.155 = f32[32,24,128]{2,1,0:T(8,128)} custom-call(f32[512,512]{1,0:T(8,128)} %features_hbm, f32[3,512]{1,0:T(4,128)} %places_ref.11, f32[2,512]{1,0:T(2,128)} %bitcast.5, s32[3,8]{1,0:T(4,128)} %anchor_ref.1, s32[1,2,3]{2,1,0:T(2,128)} %exports_ref.5), custom_call_target="tpu_custom_call" | custom-call | tf_op jit(solution)/shard_map/pallas_call | solution.py:787
  19.5 6.5 %shard_map.156 = (f32[512,512]{1,0:T(8,128)}, f32[8,512]{1,0:T(8,128)}) custom-call(f32[512,512]{1,0:T(8,128)} %features_hbm, f32[3,512]{1,0:T(4,128)} %places_ref.11, f32[512,512]{1,0:T(8,128)} %value_one_ref.3, f32[8,512]{1,0:T(8,128)} %weight_ref.5, f32[2,512]{1,0:T(2,128)} %return_ref.3, f32[512,512]{1,0:T(8,128)} %value_two_hbm.1), custom_call_target="tpu_custom_call" | custom-call | tf_op jit(solution)/shard_map/pallas_call | solution.py:797
  26.0 0.0 collective-permute-done.up_ref
  26.0 0.0 copy-start.2
  26.0 0.0 collective-permute-done.1.down_ref
  26.0 0.0 copy-start.3
  26.1 3.8 %all-to-all-start = ((f32[32,24,128]{2,1,0:T(8,128)}), f32[32,24,128]{2,1,0:T(8,128)S(1)}, u32[]{:S(2)}, u32[]{:S(2)}) async-start(f32[32,24,128]{2,1,0:T(8,128)} %shard_map.155), calls=%async_computation | async-start | bytes 786432 | tf_op jit(solution)/shard_map/all_to_all | solution.py:807
  29.9 0.0 copy-done.2
  29.9 0.0 copy-done.3
  29.9 11.2 %shard_map.157 = (f32[512,512]{1,0:T(8,128)}, f32[512,512]{1,0:T(8,128)}, f32[192,512]{1,0:T(8,128)}, f32[192,512]{1,0:T(8,128)}, f32[8,512]{1,0:T(8,128)}) custom-call(f32[200,512]{1,0:T(8,128)} %copy-done.2, f32[200,512]{1,0:T(8,128)} %copy-done.3, f32[3,512]{1,0:T(4,128)} %places_ref.11, f32[512,512]{1,0:T(8,128)} %value_one_ref.3, f32[8,512]{1,0:T(8,128)} %weight_ref.5, ...), custom_call_target="tpu_custom_call" | custom-call | tf_op jit(solution)/shard_map/pallas_call | solution.py:809
  41.1 1.8 %collective-permute-start.2 = (f32[192,512]{1,0:T(8,128)}, f32[192,512]{1,0:T(8,128)S(1)}, u32[]{:S(2)}, u32[]{:S(2)}) collective-permute-start(f32[192,512]{1,0:T(8,128)} %get-tuple-element.42), channel_id=1, source_target_pairs={{0,1},{1,2},{2,3},{3,4},{4,5},{5,6},{6,7},{7,8},{8,9},{9,10},{10,1... | collective-permute-start | bytes 1179656 | tf_op jit(solution)/shard_map/ppermute | solution.py:776
  42.9 3.7 %collective-permute-start.3 = (f32[192,512]{1,0:T(8,128)}, f32[192,512]{1,0:T(8,128)S(1)}, u32[]{:S(2)}, u32[]{:S(2)}) collective-permute-start(f32[192,512]{1,0:T(8,128)} %get-tuple-element.43), channel_id=1, source_target_pairs={{0,31},{1,0},{2,1},{3,2},{4,3},{5,4},{6,5},{7,6},{8,7},{9,8},{10,9... | collective-permute-start | bytes 1179656 | tf_op jit(solution)/shard_map/ppermute | solution.py:776
  46.6 0.0 all-to-all-done.payload_ref
  46.6 0.0 copy-start
  46.6 0.7 slice_convert_fusion
  47.3 0.1 copy-done
  47.4 21.8 %shard_map.158 = f32[32,16,128]{2,1,0:T(8,128)} custom-call(s32[32,8]{1,0:T(8,128)} %bitcast.4, f32[32,24,128]{2,1,0:T(8,128)} %copy-done, f32[12,2,2,192,96]{4,3,2,1,0:T(8,128)} %bitcast.3, bf16[192,576]{1,0:T(8,128)(2,1)} %constant.4.clone.forward_ref, bf16[192,576]{1,0:T(8,128)(2,1)} %constant.5.clone.back_ref), custom_call_target="tpu_custom_call" | custom-call | tf_op jit(solution)/shard_map/pallas_call | solution.py:834
  69.2 0.0 collective-permute-done.2.up_two_ref
  69.2 0.0 copy-start.4
  69.2 0.0 collective-permute-done.3.down_two_ref
  69.2 0.0 copy-start.5
  69.3 2.8 %all-to-all-start.1 = ((f32[32,16,128]{2,1,0:T(8,128)}), f32[32,16,128]{2,1,0:T(8,128)S(1)}, u32[]{:S(2)}, u32[]{:S(2)}) async-start(f32[32,16,128]{2,1,0:T(8,128)} %shard_map.158), calls=%async_computation.1 | async-start | bytes 524288 | tf_op jit(solution)/shard_map/all_to_all | solution.py:839
  72.1 0.0 copy-done.4
  72.1 0.0 copy-done.5
  72.1 10.9 %shard_map.159.messages_hbm = f32[512,512]{1,0:T(8,128)} custom-call(f32[512,512]{1,0:T(8,128)} %get-tuple-element.47.values_ref, f32[192,512]{1,0:T(8,128)} %copy-done.4, f32[192,512]{1,0:T(8,128)} %copy-done.5, f32[8,512]{1,0:T(8,128)} %get-tuple-element.45.ghost_places_ref, f32[3,512]{1,0:T(4,128)} %places_ref.11, f32[8,512]{1,0:T(8,128)} %weight_ref.7), custom_call_target="tpu_custom_call" | custom-call | tf_op jit(solution)/shard_map/pallas_call | solution.py:841
  83.0 0.0 all-to-all-done.1.received_ref
  83.0 0.0 copy-start.1
  83.0 0.7 copy-done.1
  83.7 6.0 %shard_map.160 = f32[512,512]{1,0:T(8,128)} custom-call(f32[32,16,128]{2,1,0:T(8,128)} %copy-done.1, f32[8,512]{1,0:T(8,128)} %get-tuple-element.45.ghost_places_ref, f32[3,512]{1,0:T(4,128)} %places_ref.11, f32[8,512]{1,0:T(8,128)} %weight_ref.7, f32[2,512]{1,0:T(2,128)} %return_ref.3, f32[8,512]{1,0:T(8,128)} %get-tuple-element.46.returned_ref, ...), custom_call_target="tpu_custom_call" | custom-call | tf_op jit(solution)/shard_map/pallas_call | solution.py:850
Async XLA Ops:
  2.7 23.3 %collective-permute-start = (f32[200,512]{1,0:T(8,128)}, f32[200,512]{1,0:T(8,128)S(1)}, u32[]{:S(2)}, u32[]{:S(2)}) collective-permute-start(f32[200,512]{1,0:T(8,128)} %get-tuple-element.33), channel_id=1, source_target_pairs={{0,1},{1,2},{2,3},{3,4},{4,5},{5,6},{6,7},{7,8},{8,9},{9,10},{10,1... | collective-permute-start | bytes 1228808 | tf_op jit(solution)/shard_map/ppermute | solution.py:776
  5.7 20.4 %collective-permute-start.1 = (f32[200,512]{1,0:T(8,128)}, f32[200,512]{1,0:T(8,128)S(1)}, u32[]{:S(2)}, u32[]{:S(2)}) collective-permute-start(f32[200,512]{1,0:T(8,128)} %get-tuple-element.34), channel_id=1, source_target_pairs={{0,31},{1,0},{2,1},{3,2},{4,3},{5,4},{6,5},{7,6},{8,7},{9,8},{10,9... | collective-permute-start | bytes 1228808 | tf_op jit(solution)/shard_map/ppermute | solution.py:776
  26.0 3.9 %copy-start.2 = (f32[200,512]{1,0:T(8,128)}, f32[200,512]{1,0:T(8,128)S(1)}, u32[]{:S(2)}) copy-start(f32[200,512]{1,0:T(8,128)S(1)} %collective-permute-done.up_ref) | copy-start | bytes 1228804
  26.0 3.9 %copy-start.3 = (f32[200,512]{1,0:T(8,128)}, f32[200,512]{1,0:T(8,128)S(1)}, u32[]{:S(2)}) copy-start(f32[200,512]{1,0:T(8,128)S(1)} %collective-permute-done.1.down_ref) | copy-start | bytes 1228804
  26.1 20.6 %all-to-all-start = ((f32[32,24,128]{2,1,0:T(8,128)}), f32[32,24,128]{2,1,0:T(8,128)S(1)}, u32[]{:S(2)}, u32[]{:S(2)}) async-start(f32[32,24,128]{2,1,0:T(8,128)} %shard_map.155), calls=%async_computation | async-start | bytes 786432 | tf_op jit(solution)/shard_map/all_to_all | solution.py:807
  41.1 28.1 %collective-permute-start.2 = (f32[192,512]{1,0:T(8,128)}, f32[192,512]{1,0:T(8,128)S(1)}, u32[]{:S(2)}, u32[]{:S(2)}) collective-permute-start(f32[192,512]{1,0:T(8,128)} %get-tuple-element.42), channel_id=1, source_target_pairs={{0,1},{1,2},{2,3},{3,4},{4,5},{5,6},{6,7},{7,8},{8,9},{9,10},{10,1... | collective-permute-start | bytes 1179656 | tf_op jit(solution)/shard_map/ppermute | solution.py:776
  42.9 26.3 %collective-permute-start.3 = (f32[192,512]{1,0:T(8,128)}, f32[192,512]{1,0:T(8,128)S(1)}, u32[]{:S(2)}, u32[]{:S(2)}) collective-permute-start(f32[192,512]{1,0:T(8,128)} %get-tuple-element.43), channel_id=1, source_target_pairs={{0,31},{1,0},{2,1},{3,2},{4,3},{5,4},{6,5},{7,6},{8,7},{9,8},{10,9... | collective-permute-start | bytes 1179656 | tf_op jit(solution)/shard_map/ppermute | solution.py:776
  46.6 0.8 copy-start
  69.2 2.9 %copy-start.4 = (f32[192,512]{1,0:T(8,128)}, f32[192,512]{1,0:T(8,128)S(1)}, u32[]{:S(2)}) copy-start(f32[192,512]{1,0:T(8,128)S(1)} %collective-permute-done.2.up_two_ref) | copy-start | bytes 1179652
  69.2 2.9 %copy-start.5 = (f32[192,512]{1,0:T(8,128)}, f32[192,512]{1,0:T(8,128)S(1)}, u32[]{:S(2)}) copy-start(f32[192,512]{1,0:T(8,128)S(1)} %collective-permute-done.3.down_two_ref) | copy-start | bytes 1179652
  69.3 13.7 %all-to-all-start.1 = ((f32[32,16,128]{2,1,0:T(8,128)}), f32[32,16,128]{2,1,0:T(8,128)S(1)}, u32[]{:S(2)}, u32[]{:S(2)}) async-start(f32[32,16,128]{2,1,0:T(8,128)} %shard_map.158), calls=%async_computation.1 | async-start | bytes 524288 | tf_op jit(solution)/shard_map/all_to_all | solution.py:839
  83.0 0.7 copy-start.1
